TPU v7x, 512 devices: a whole 4x4x16 slice. The times are simulated.
512 devices in a mesh: gx: 16 (over z_lo, core), gy: 4 (over x), gz: 8 (over z_hi, y).
Axes of the slice: x: 4, y: 4, z: 16 (z_hi: 2, z_lo: 8; z = z_hi * 8 + z_lo), core: 2. Of those that a mesh axis runs over, the one named last changes fastest.
Arguments:
- velocity: float32 [3, 5242880], P(None, ('gx', 'gy', 'gz')), may hold values from -6 to 6
- position: int32 [2, 3, 5242880], P(None, None, ('gx', 'gy', 'gz')), may hold values from 0 to 511, as said below
- bead_velocity: float32 [3, 524288], P(None, ('gx', 'gy', 'gz')), may hold values from -6 to 6
- bead_mass: float32 [524288], P(('gx', 'gy', 'gz')), may hold values from 1 to 10
- bead_position: int32 [2, 3, 524288], P(None, None, ('gx', 'gy', 'gz')), may hold values from 0 to 511, as said below
- grid_shift: int32 [2, 3], replicated, may hold values from -8 to 8, as said below
- rot_axis: int32 [2, 64, 128, 128], P(None, 'gx', 'gy', 'gz'), may hold values from 0 to 63
- leave_count: int32 [3, 2, 512], P(None, None, ('gx', 'gy', 'gz')), may hold values from 1 to 256, as said below
- leave_index: int32 [3, 2, 131072], P(None, None, ('gx', 'gy', 'gz')), may hold values from -1 to 10239, as said below
Outputs:
- velocity_out: float32 [3, 5242880], P(None, ('gx', 'gy', 'gz'))
- bead_out: float32 [3, 524288], P(None, ('gx', 'gy', 'gz'))
- arrivals: float32 [3, 2, 3, 131072], P(None, None, None, ('gx', 'gy', 'gz'))
Inputs may be any that keep to these rules, and one draw needn't show every extreme that they name: `position`: coordinates of a device's own particles: along the dimensions 0 to 63, 0 to 511 and 0 to 255. `bead_position`: coordinates of a device's own beads, in the same ranges as the particles. `grid_shift`: never zero; along each dimension the two steps shift in opposite directions, and along one dimension both by 8. `leave_count`: for every dimension and side, some device's count is exactly 256. `leave_index`: entries before a face's count are indices of the device's own particles; the rest are -1.
All inputs are finite; a program needn't handle non-finite values.
Results may differ from a plain program's by a relative error of at most 0.00013.
Values sent between devices are 32-bit elements; how exact they have to be, the bound alone decides.
A program may use at most 64 MiB of HBM per device.

v0:
```python
import math

import jax
import jax.numpy as jnp
from jax import lax
from jax.sharding import PartitionSpec as P

STEPS = 2
SUB = 16
AXES = 64
CAP = 256


COSINE = math.cos(130.0 * math.pi / 180.0)
SINE = math.sin(130.0 * math.pi / 180.0)
GOLDEN = math.pi * (3.0 - math.sqrt(5.0))


def with_halo(x, sides, width):
    for axis, dim in sides:
        count, length = (lax.axis_size(axis), x.shape[dim])
        up = [(i, (i + 1) % count) for i in range(count)]
        down = [(j, i) for i, j in up]
        last = lax.slice_in_dim(x, length - width, length, axis=dim)
        leading = lax.slice_in_dim(x, 0, width, axis=dim)
        before = lax.ppermute(last, axis, up)
        after = lax.ppermute(leading, axis, down)
        x = jnp.concatenate([before, x, after], axis=dim)
    return x


def axis_table():
    ordinal = jnp.arange(AXES, dtype=jnp.float32) + 0.5
    height = 1.0 - 2.0 * ordinal / AXES
    radius = jnp.sqrt(1.0 - height * height)
    turning = ordinal * GOLDEN
    return jnp.stack([radius * jnp.cos(turning), radius * jnp.sin(turning), height])


def rotation_rows(table, indices):
    flat_index = indices.reshape(-1)
    onehot = (flat_index[None, :] == jnp.arange(AXES, dtype=jnp.int32)[:, None]).astype(jnp.float32)
    normal = jnp.dot(table, onehot, precision=lax.Precision.HIGHEST)
    axis_one = normal[0]
    axis_two = normal[1]
    axis_three = normal[2]
    rest = 1.0 - COSINE
    entries = [
        COSINE + rest * axis_one * axis_one,
        -SINE * axis_three + rest * axis_one * axis_two,
        SINE * axis_two + rest * axis_one * axis_three,
        SINE * axis_three + rest * axis_two * axis_one,
        COSINE + rest * axis_two * axis_two,
        -SINE * axis_one + rest * axis_two * axis_three,
        -SINE * axis_two + rest * axis_three * axis_one,
        SINE * axis_one + rest * axis_three * axis_two,
        COSINE + rest * axis_three * axis_three,
    ]
    return jnp.stack(entries).reshape((9,) + indices.shape)


def extended_cells(coords, shift, extent):
    layer_first = jnp.floor_divide(coords[0] - shift[0], SUB) + 1
    layer_second = jnp.floor_divide(coords[1] - shift[1], SUB) + 1
    layer_third = jnp.floor_divide(coords[2] - shift[2], SUB) + 1
    return (layer_first * extent[1] + layer_second) * extent[2] + layer_third


def fold_owned(stacked, axis_dim):
    owned_length = stacked.shape[axis_dim] - 4
    lower_face = lax.slice_in_dim(stacked, 0, 1, axis=axis_dim)
    upper_face = lax.slice_in_dim(stacked, owned_length + 3, owned_length + 4, axis=axis_dim)
    first_layer = lax.slice_in_dim(stacked, 2, 3, axis=axis_dim) + lower_face
    middle = lax.slice_in_dim(stacked, 3, owned_length + 1, axis=axis_dim)
    last_layer = (
        lax.slice_in_dim(stacked, owned_length + 1, owned_length + 2, axis=axis_dim) + upper_face
    )
    return jnp.concatenate([first_layer, middle, last_layer], axis=axis_dim)


def collide(moving, gathered):
    mean_part = gathered[:3]
    relative = moving - mean_part
    turned = jnp.stack(
        [
            gathered[3 + 3 * row_index] * relative[0]
            + gathered[4 + 3 * row_index] * relative[1]
            + gathered[5 + 3 * row_index] * relative[2]
            for row_index in range(3)
        ]
    )
    return mean_part + turned


def per_device(
    velocity,
    position,
    bead_velocity,
    bead_mass,
    bead_position,
    grid_shift,
    rot_axis,
    leave_count,
    leave_index,
):
    size_first = rot_axis.shape[1]
    size_second = rot_axis.shape[2]
    size_third = rot_axis.shape[3]
    extent = (size_first + 2, size_second + 2, size_third + 2)
    cells_extended = extent[0] * extent[1] * extent[2]
    solvent_count = velocity.shape[1]
    table = axis_table()
    weights = jnp.concatenate([jnp.ones((solvent_count,), jnp.float32), bead_mass])
    for step_index in range(STEPS):
        shift = grid_shift[step_index]
        all_cells = jnp.concatenate(
            [
                extended_cells(position[step_index], shift, extent),
                extended_cells(bead_position[step_index], shift, extent),
            ]
        )
        moving = jnp.concatenate([velocity, bead_velocity], axis=1)
        summands = jnp.concatenate([weights[None], moving * weights[None]], axis=0)
        totals = jax.vmap(
            lambda values: jax.ops.segment_sum(values, all_cells, num_segments=cells_extended)
        )(summands)
        totals = totals.reshape((4,) + extent)
        widened = with_halo(totals, (("gx", 1), ("gy", 2), ("gz", 3)), 1)
        owned = fold_owned(fold_owned(fold_owned(widened, 1), 2), 3)
        means = owned[1:] / jnp.maximum(owned[0], 1.0)[None]
        results = jnp.concatenate([means, rotation_rows(table, rot_axis[step_index])], axis=0)
        beside_all = with_halo(results, (("gx", 1), ("gy", 2), ("gz", 3)), 1)
        flat_results = beside_all.reshape(12, cells_extended)
        gathered = jnp.take(flat_results, all_cells, axis=1)
        moving = collide(moving, gathered)
        velocity = moving[:, :solvent_count]
        bead_velocity = moving[:, solvent_count:]
    slot_number = jnp.arange(CAP, dtype=jnp.int32)
    usable = slot_number[None, None, :] < leave_count
    chosen = jnp.take(velocity, jnp.maximum(leave_index, 0).reshape(-1), axis=1).reshape(
        3, 3, 2, CAP
    )
    chosen = jnp.where(usable[None], chosen, 0.0)
    outbox = jnp.transpose(chosen, (1, 2, 0, 3))
    across_first = with_halo(outbox[0], (("gx", 0),), 1)
    across_second = with_halo(outbox[1], (("gy", 0),), 1)
    across_third = with_halo(outbox[2], (("gz", 0),), 1)
    arrivals = jnp.stack(
        [
            jnp.stack([across_first[0], across_first[3]]),
            jnp.stack([across_second[0], across_second[3]]),
            jnp.stack([across_third[0], across_third[3]]),
        ]
    )
    return (velocity, bead_velocity, arrivals)


def solution(mesh):
    return jax.shard_map(
        per_device,
        mesh=mesh,
        in_specs=(
            P(None, ("gx", "gy", "gz")),
            P(None, None, ("gx", "gy", "gz")),
            P(None, ("gx", "gy", "gz")),
            P(("gx", "gy", "gz")),
            P(None, None, ("gx", "gy", "gz")),
            P(),
            P(None, "gx", "gy", "gz"),
            P(None, None, ("gx", "gy", "gz")),
            P(None, None, ("gx", "gy", "gz")),
        ),
        out_specs=(
            P(None, ("gx", "gy", "gz")),
            P(None, ("gx", "gy", "gz")),
            P(None, None, None, ("gx", "gy", "gz")),
        ),
        check_vma=False,
    )
```

profile of v0, /device:TPU:24, one launch (start us, length us, event | category | flops | bytes accessed | tf_op | source)
XLA Modules:
  0.0 481.2 jit_solution(4779725689077661225)
XLA Ops:
  2.2 5.1 %slice_subtract_fusion.2 = (s32[1,1,10240]{2,0,1:T(1,128)S(1)}, s32[1,1,10240]{2,0,1:T(1,128)S(1)}, s32[1,1,10240]{2,0,1:T(1,128)S(1)}, s32[1,1,10240]{2,0,1:T(1...) fusion(s32[2,3,10240]{2,0,1:T(2,128)} %param.12, s32[]{:T(128)} %bitcast.14, s32[]{:T(128)} %bitcast.10, ...), kind=kLoop, calls=%fused_computation.167 | loop fusion | flops 61440 | bytes 491544 | tf_op jit(solution)/shard_map/sub | solution.py:65
  7.2 4.6 slice_subtract_fusion.8
  18.5 61.0 %scatter_custom_fusion = f32[4,3672]{0,1:T(8,128)S(1)} fusion(s32[11264]{0:T(1024)S(1)} %get-tuple-element.85, f32[11264,4]{1,0:T(8,128)} %copy.234, f32[]{:T(128)} %constant.138.clone.1), kind=kCustom, calls=%fused_computation.7 | custom fusion | flops 45056 | bytes 59264 | tf_op jit(solution)/shard_map/vmap()/scatter-add | solution.py:125
  82.4 12.6 %collective-permute-start.1 = (f32[4,1,34,18]{3,2,1,0:T(8,128)S(1)}, f32[4,1,34,18]{3,2,1,0:T(8,128)S(1)}, u32[]{:S(2)}, u32[]{:S(2)}) collective-permute-start(f32[4,1,34,18]{3,2,1,0:T(8,128)S(1)} %get-tuple-element.53), channel_id=1, source_target_pairs={{32,0},{64,32},{96,64},{128,96},{160,128},{192,160},{224,192},{256... | collective-permute-start | bytes 29384 | tf_op jit(solution)/shard_map/ppermute | solution.py:27
  109.8 13.0 %collective-permute-start.4 = (f32[4,8,36,1]{2,1,3,0:T(8,128)S(1)}, f32[4,8,36,1]{2,1,3,0:T(8,128)S(1)}, u32[]{:S(2)}, u32[]{:S(2)}) collective-permute-start(f32[4,8,36,1]{2,1,3,0:T(8,128)S(1)} %get-tuple-element.66), channel_id=1, source_target_pairs={{0,1},{1,2},{2,3},{3,4},{4,5},{5,6},{6,7},{7,0},{8,9},{9,10},{10,1... | collective-permute-start | bytes 13832 | tf_op jit(solution)/shard_map/ppermute | solution.py:26
  127.4 12.0 %collective-permute-done.5 = f32[4,8,36,1]{2,1,3,0:T(8,128)S(1)} collective-permute-done((f32[4,8,36,1]{2,1,3,0:T(8,128)S(1)}, f32[4,8,36,1]{2,1,3,0:T(8,128)S(1)}, u32[]{:S(2)}, u32[]{:S(2)}) %collective-permute-start.5) | collective-permute-done | bytes 4640 | tf_op jit(solution)/shard_map/ppermute | solution.py:27
  142.4 10.2 %collective-permute-start.7 = (f32[12,1,32,16]{2,3,1,0:T(8,128)S(1)}, f32[12,1,32,16]{2,3,1,0:T(8,128)S(1)}, u32[]{:S(2)}, u32[]{:S(2)}) collective-permute-start(f32[12,1,32,16]{2,3,1,0:T(8,128)S(1)} %get-tuple-element.61), channel_id=1, source_target_pairs={{32,0},{64,32},{96,64},{128,96},{160,128},{192,160},{224,192},{256... | collective-permute-start | bytes 73736 | tf_op jit(solution)/shard_map/ppermute | solution.py:27
  172.3 13.3 %collective-permute-done.11 = f32[12,6,34,1]{2,3,1,0:T(1,128)S(1)} collective-permute-done((f32[12,6,34,1]{2,3,1,0:T(1,128)S(1)}, f32[12,6,34,1]{2,3,1,0:T(1,128)S(1)}, u32[]{:S(2)}, u32[]{:S(2)}) %collective-permute-start.11) | collective-permute-done | bytes 9824 | tf_op jit(solution)/shard_map/ppermute | solution.py:27
  187.9 38.0 %gather_fusion.1 = f32[11264,12]{1,0:T(8,128)} fusion(f32[12,3672]{0,1:T(8,128)S(1)} %copy.257, s32[11264]{0:T(1024)S(1)} %get-tuple-element.84), kind=kCustom, calls=%fused_computation.clone | custom fusion | bytes 1126400 | tf_op jit(solution)/shard_map/jit(_take)/gather | solution.py:134
  225.9 4.5 copy.258
  235.3 61.0 %scatter_custom_fusion.1 = f32[4,3672]{0,1:T(8,128)S(1)} fusion(s32[11264]{0:T(1024)S(1)} %get-tuple-element.106, f32[11264,4]{1,0:T(8,128)} %copy.259, f32[]{:T(128)} %constant.138.clone.1), kind=kCustom, calls=%fused_computation.5 | custom fusion | flops 45056 | bytes 59264 | tf_op jit(solution)/shard_map/vmap()/scatter-add | solution.py:125
  299.1 10.2 %collective-permute-start.13 = (f32[4,1,34,18]{3,2,1,0:T(8,128)S(1)}, f32[4,1,34,18]{3,2,1,0:T(8,128)S(1)}, u32[]{:S(2)}, u32[]{:S(2)}) collective-permute-start(f32[4,1,34,18]{3,2,1,0:T(8,128)S(1)} %get-tuple-element.51), channel_id=1, source_target_pairs={{32,0},{64,32},{96,64},{128,96},{160,128},{192,160},{224,192},{256... | collective-permute-start | bytes 29384 | tf_op jit(solution)/shard_map/ppermute | solution.py:27
  314.9 3.9 collective-permute-start.15
  325.8 3.9 collective-permute-start.17
  331.4 10.9 %collective-permute-done.17 = f32[4,8,36,1]{2,1,3,0:T(8,128)S(1)} collective-permute-done((f32[4,8,36,1]{2,1,3,0:T(8,128)S(1)}, f32[4,8,36,1]{2,1,3,0:T(8,128)S(1)}, u32[]{:S(2)}, u32[]{:S(2)}) %collective-permute-start.17) | collective-permute-done | bytes 4640 | tf_op jit(solution)/shard_map/ppermute | solution.py:27
  345.3 10.2 %collective-permute-start.19 = (f32[12,1,32,16]{2,3,1,0:T(8,128)S(1)}, f32[12,1,32,16]{2,3,1,0:T(8,128)S(1)}, u32[]{:S(2)}, u32[]{:S(2)}) collective-permute-start(f32[12,1,32,16]{2,3,1,0:T(8,128)S(1)} %get-tuple-element.59), channel_id=1, source_target_pairs={{32,0},{64,32},{96,64},{128,96},{160,128},{192,160},{224,192},{256... | collective-permute-start | bytes 73736 | tf_op jit(solution)/shard_map/ppermute | solution.py:27
  371.5 4.1 collective-permute-start.23
  376.3 11.9 %collective-permute-done.23 = f32[12,6,34,1]{2,3,1,0:T(1,128)S(1)} collective-permute-done((f32[12,6,34,1]{2,3,1,0:T(1,128)S(1)}, f32[12,6,34,1]{2,3,1,0:T(1,128)S(1)}, u32[]{:S(2)}, u32[]{:S(2)}) %collective-permute-start.23) | collective-permute-done | bytes 9824 | tf_op jit(solution)/shard_map/ppermute | solution.py:27
  390.5 38.0 %gather_fusion.2 = f32[11264,12]{1,0:T(8,128)} fusion(f32[12,3672]{0,1:T(8,128)S(1)} %copy.282, s32[11264]{0:T(1024)S(1)} %copy-done.5), kind=kCustom, calls=%fused_computation.1.clone | custom fusion | bytes 1126400 | tf_op jit(solution)/shard_map/jit(_take)/gather | solution.py:134
  428.5 4.5 copy.283
  437.0 5.1 %gather_fusion = f32[1536,3]{1,0:T(8,128)S(1)} fusion(f32[3,10240]{0,1:T(8,128)} %copy.285, s32[2048]{0:T(1024)S(1)} %pad_clamp_fusion), kind=kCustom, calls=%fused_computation.2 | custom fusion | bytes 43008 | tf_op jit(solution)/shard_map/jit(_take)/gather | solution.py:140
  444.4 10.2 %collective-permute-start.25 = (f32[1,3,256]{2,0,1:T(1,128)S(1)}, f32[1,3,256]{2,0,1:T(1,128)S(1)}, u32[]{:S(2)}, u32[]{:S(2)}) collective-permute-start(f32[1,3,256]{2,0,1:T(1,128)S(1)} %get-tuple-element.93), channel_id=1, source_target_pairs={{32,0},{64,32},{96,64},{128,96},{160,128},{192,160},{224,192},{256... | collective-permute-start | bytes 9224 | tf_op jit(solution)/shard_map/ppermute | solution.py:27
  464.3 3.9 collective-permute-start.29
  468.3 12.3 %collective-permute-done.29 = f32[1,3,256]{2,0,1:T(1,128)S(1)} collective-permute-done((f32[1,3,256]{2,0,1:T(1,128)S(1)}, f32[1,3,256]{2,0,1:T(1,128)S(1)}, u32[]{:S(2)}, u32[]{:S(2)}) %collective-permute-start.29) | collective-permute-done | bytes 3104 | tf_op jit(solution)/shard_map/ppermute | solution.py:27
  (253 shorter events, 114.5 us)
Async XLA Ops:
  80.4 15.6 %collective-permute-start = (f32[4,1,34,18]{3,2,1,0:T(8,128)S(1)}, f32[4,1,34,18]{3,2,1,0:T(8,128)S(1)}, u32[]{:S(2)}, u32[]{:S(2)}) collective-permute-start(f32[4,1,34,18]{3,2,1,0:T(8,128)S(1)} %get-tuple-element.52), channel_id=1, source_target_pairs={{0,32},{32,64},{64,96},{96,128},{128,160},{160,192},{192,224},{224... | collective-permute-start | bytes 29384 | tf_op jit(solution)/shard_map/ppermute | solution.py:26
  82.4 14.6 %collective-permute-start.1 = (f32[4,1,34,18]{3,2,1,0:T(8,128)S(1)}, f32[4,1,34,18]{3,2,1,0:T(8,128)S(1)}, u32[]{:S(2)}, u32[]{:S(2)}) collective-permute-start(f32[4,1,34,18]{3,2,1,0:T(8,128)S(1)} %get-tuple-element.53), channel_id=1, source_target_pairs={{32,0},{64,32},{96,64},{128,96},{160,128},{192,160},{224,192},{256... | collective-permute-start | bytes 29384 | tf_op jit(solution)/shard_map/ppermute | solution.py:27
  97.4 9.8 %collective-permute-start.2 = (f32[4,8,1,18]{2,1,3,0:T(8,128)S(1)}, f32[4,8,1,18]{2,1,3,0:T(8,128)S(1)}, u32[]{:S(2)}, u32[]{:S(2)}) collective-permute-start(f32[4,8,1,18]{2,1,3,0:T(8,128)S(1)} %get-tuple-element.68), channel_id=1, source_target_pairs={{0,8},{8,16},{16,24},{24,0},{1,9},{9,17},{17,25},{25,1},{2,10},{10... | collective-permute-start | bytes 6920 | tf_op jit(solution)/shard_map/ppermute | solution.py:26
  100.8 8.6 %collective-permute-start.3 = (f32[4,8,1,18]{2,1,3,0:T(8,128)S(1)}, f32[4,8,1,18]{2,1,3,0:T(8,128)S(1)}, u32[]{:S(2)}, u32[]{:S(2)}) collective-permute-start(f32[4,8,1,18]{2,1,3,0:T(8,128)S(1)} %get-tuple-element.69), channel_id=1, source_target_pairs={{8,0},{16,8},{24,16},{0,24},{9,1},{17,9},{25,17},{1,25},{10,2},{18... | collective-permute-start | bytes 6920 | tf_op jit(solution)/shard_map/ppermute | solution.py:27
  109.8 17.6 %collective-permute-start.4 = (f32[4,8,36,1]{2,1,3,0:T(8,128)S(1)}, f32[4,8,36,1]{2,1,3,0:T(8,128)S(1)}, u32[]{:S(2)}, u32[]{:S(2)}) collective-permute-start(f32[4,8,36,1]{2,1,3,0:T(8,128)S(1)} %get-tuple-element.66), channel_id=1, source_target_pairs={{0,1},{1,2},{2,3},{3,4},{4,5},{5,6},{6,7},{7,0},{8,9},{9,10},{10,1... | collective-permute-start | bytes 13832 | tf_op jit(solution)/shard_map/ppermute | solution.py:26
  122.8 16.6 %collective-permute-start.5 = (f32[4,8,36,1]{2,1,3,0:T(8,128)S(1)}, f32[4,8,36,1]{2,1,3,0:T(8,128)S(1)}, u32[]{:S(2)}, u32[]{:S(2)}) collective-permute-start(f32[4,8,36,1]{2,1,3,0:T(8,128)S(1)} %get-tuple-element.67), channel_id=1, source_target_pairs={{1,0},{2,1},{3,2},{4,3},{5,4},{6,5},{7,6},{0,7},{9,8},{10,9},{11,1... | collective-permute-start | bytes 13832 | tf_op jit(solution)/shard_map/ppermute | solution.py:27
  140.5 13.3 %collective-permute-start.6 = (f32[12,1,32,16]{2,3,1,0:T(8,128)S(1)}, f32[12,1,32,16]{2,3,1,0:T(8,128)S(1)}, u32[]{:S(2)}, u32[]{:S(2)}) collective-permute-start(f32[12,1,32,16]{2,3,1,0:T(8,128)S(1)} %get-tuple-element.60), channel_id=1, source_target_pairs={{0,32},{32,64},{64,96},{96,128},{128,160},{160,192},{192,224},{224... | collective-permute-start | bytes 73736 | tf_op jit(solution)/shard_map/ppermute | solution.py:26
  142.4 12.4 %collective-permute-start.7 = (f32[12,1,32,16]{2,3,1,0:T(8,128)S(1)}, f32[12,1,32,16]{2,3,1,0:T(8,128)S(1)}, u32[]{:S(2)}, u32[]{:S(2)}) collective-permute-start(f32[12,1,32,16]{2,3,1,0:T(8,128)S(1)} %get-tuple-element.61), channel_id=1, source_target_pairs={{32,0},{64,32},{96,64},{128,96},{160,128},{192,160},{224,192},{256... | collective-permute-start | bytes 73736 | tf_op jit(solution)/shard_map/ppermute | solution.py:27
  155.6 7.6 %collective-permute-start.8 = (f32[12,6,1,16]{3,2,1,0:T(1,128)S(1)}, f32[12,6,1,16]{3,2,1,0:T(1,128)S(1)}, u32[]{:S(2)}, u32[]{:S(2)}) collective-permute-start(f32[12,6,1,16]{3,2,1,0:T(1,128)S(1)} %copy.252), channel_id=1, source_target_pairs={{0,8},{8,16},{16,24},{24,0},{1,9},{9,17},{17,25},{25,1},{2,10},{10... | collective-permute-start | bytes 13832 | tf_op jit(solution)/shard_map/ppermute | solution.py:26
  169.0 16.7 %collective-permute-start.11 = (f32[12,6,34,1]{2,3,1,0:T(1,128)S(1)}, f32[12,6,34,1]{2,3,1,0:T(1,128)S(1)}, u32[]{:S(2)}, u32[]{:S(2)}) collective-permute-start(f32[12,6,34,1]{2,3,1,0:T(1,128)S(1)} %get-tuple-element.35), channel_id=1, source_target_pairs={{1,0},{2,1},{3,2},{4,3},{5,4},{6,5},{7,6},{0,7},{9,8},{10,9},{11,1... | collective-permute-start | bytes 29384 | tf_op jit(solution)/shard_map/ppermute | solution.py:27
  297.1 13.1 %collective-permute-start.12 = (f32[4,1,34,18]{3,2,1,0:T(8,128)S(1)}, f32[4,1,34,18]{3,2,1,0:T(8,128)S(1)}, u32[]{:S(2)}, u32[]{:S(2)}) collective-permute-start(f32[4,1,34,18]{3,2,1,0:T(8,128)S(1)} %get-tuple-element.50), channel_id=1, source_target_pairs={{0,32},{32,64},{64,96},{96,128},{128,160},{160,192},{192,224},{224... | collective-permute-start | bytes 29384 | tf_op jit(solution)/shard_map/ppermute | solution.py:26
  299.1 12.3 %collective-permute-start.13 = (f32[4,1,34,18]{3,2,1,0:T(8,128)S(1)}, f32[4,1,34,18]{3,2,1,0:T(8,128)S(1)}, u32[]{:S(2)}, u32[]{:S(2)}) collective-permute-start(f32[4,1,34,18]{3,2,1,0:T(8,128)S(1)} %get-tuple-element.51), channel_id=1, source_target_pairs={{32,0},{64,32},{96,64},{128,96},{160,128},{192,160},{224,192},{256... | collective-permute-start | bytes 29384 | tf_op jit(solution)/shard_map/ppermute | solution.py:27
  311.8 9.8 %collective-permute-start.14 = (f32[4,8,1,18]{2,1,3,0:T(8,128)S(1)}, f32[4,8,1,18]{2,1,3,0:T(8,128)S(1)}, u32[]{:S(2)}, u32[]{:S(2)}) collective-permute-start(f32[4,8,1,18]{2,1,3,0:T(8,128)S(1)} %get-tuple-element.64), channel_id=1, source_target_pairs={{0,8},{8,16},{16,24},{24,0},{1,9},{9,17},{17,25},{25,1},{2,10},{10... | collective-permute-start | bytes 6920 | tf_op jit(solution)/shard_map/ppermute | solution.py:26
  314.9 8.6 %collective-permute-start.15 = (f32[4,8,1,18]{2,1,3,0:T(8,128)S(1)}, f32[4,8,1,18]{2,1,3,0:T(8,128)S(1)}, u32[]{:S(2)}, u32[]{:S(2)}) collective-permute-start(f32[4,8,1,18]{2,1,3,0:T(8,128)S(1)} %get-tuple-element.65), channel_id=1, source_target_pairs={{8,0},{16,8},{24,16},{0,24},{9,1},{17,9},{25,17},{1,25},{10,2},{18... | collective-permute-start | bytes 6920 | tf_op jit(solution)/shard_map/ppermute | solution.py:27
  325.8 16.5 %collective-permute-start.17 = (f32[4,8,36,1]{2,1,3,0:T(8,128)S(1)}, f32[4,8,36,1]{2,1,3,0:T(8,128)S(1)}, u32[]{:S(2)}, u32[]{:S(2)}) collective-permute-start(f32[4,8,36,1]{2,1,3,0:T(8,128)S(1)} %get-tuple-element.63), channel_id=1, source_target_pairs={{1,0},{2,1},{3,2},{4,3},{5,4},{6,5},{7,6},{0,7},{9,8},{10,9},{11,1... | collective-permute-start | bytes 13832 | tf_op jit(solution)/shard_map/ppermute | solution.py:27
  343.4 13.4 %collective-permute-start.18 = (f32[12,1,32,16]{2,3,1,0:T(8,128)S(1)}, f32[12,1,32,16]{2,3,1,0:T(8,128)S(1)}, u32[]{:S(2)}, u32[]{:S(2)}) collective-permute-start(f32[12,1,32,16]{2,3,1,0:T(8,128)S(1)} %get-tuple-element.58), channel_id=1, source_target_pairs={{0,32},{32,64},{64,96},{96,128},{128,160},{160,192},{192,224},{224... | collective-permute-start | bytes 73736 | tf_op jit(solution)/shard_map/ppermute | solution.py:26
  345.3 12.8 %collective-permute-start.19 = (f32[12,1,32,16]{2,3,1,0:T(8,128)S(1)}, f32[12,1,32,16]{2,3,1,0:T(8,128)S(1)}, u32[]{:S(2)}, u32[]{:S(2)}) collective-permute-start(f32[12,1,32,16]{2,3,1,0:T(8,128)S(1)} %get-tuple-element.59), channel_id=1, source_target_pairs={{32,0},{64,32},{96,64},{128,96},{160,128},{192,160},{224,192},{256... | collective-permute-start | bytes 73736 | tf_op jit(solution)/shard_map/ppermute | solution.py:27
  358.9 7.6 %collective-permute-start.20 = (f32[12,6,1,16]{3,2,1,0:T(1,128)S(1)}, f32[12,6,1,16]{3,2,1,0:T(1,128)S(1)}, u32[]{:S(2)}, u32[]{:S(2)}) collective-permute-start(f32[12,6,1,16]{3,2,1,0:T(1,128)S(1)} %copy.277), channel_id=1, source_target_pairs={{0,8},{8,16},{16,24},{24,0},{1,9},{9,17},{17,25},{25,1},{2,10},{10... | collective-permute-start | bytes 13832 | tf_op jit(solution)/shard_map/ppermute | solution.py:26
  371.5 16.7 %collective-permute-start.23 = (f32[12,6,34,1]{2,3,1,0:T(1,128)S(1)}, f32[12,6,34,1]{2,3,1,0:T(1,128)S(1)}, u32[]{:S(2)}, u32[]{:S(2)}) collective-permute-start(f32[12,6,34,1]{2,3,1,0:T(1,128)S(1)} %get-tuple-element.33), channel_id=1, source_target_pairs={{1,0},{2,1},{3,2},{4,3},{5,4},{6,5},{7,6},{0,7},{9,8},{10,9},{11,1... | collective-permute-start | bytes 29384 | tf_op jit(solution)/shard_map/ppermute | solution.py:27
  442.5 21.8 %collective-permute-start.24 = (f32[1,3,256]{2,0,1:T(1,128)S(1)}, f32[1,3,256]{2,0,1:T(1,128)S(1)}, u32[]{:S(2)}, u32[]{:S(2)}) collective-permute-start(f32[1,3,256]{2,0,1:T(1,128)S(1)} %get-tuple-element.88), channel_id=1, source_target_pairs={{0,32},{32,64},{64,96},{96,128},{128,160},{160,192},{192,224},{224... | collective-permute-start | bytes 9224 | tf_op jit(solution)/shard_map/ppermute | solution.py:26
  444.4 23.8 %collective-permute-start.25 = (f32[1,3,256]{2,0,1:T(1,128)S(1)}, f32[1,3,256]{2,0,1:T(1,128)S(1)}, u32[]{:S(2)}, u32[]{:S(2)}) collective-permute-start(f32[1,3,256]{2,0,1:T(1,128)S(1)} %get-tuple-element.93), channel_id=1, source_target_pairs={{32,0},{64,32},{96,64},{128,96},{160,128},{192,160},{224,192},{256... | collective-permute-start | bytes 9224 | tf_op jit(solution)/shard_map/ppermute | solution.py:27
  455.3 13.0 %collective-permute-start.26 = (f32[1,3,256]{2,0,1:T(1,128)S(1)}, f32[1,3,256]{2,0,1:T(1,128)S(1)}, u32[]{:S(2)}, u32[]{:S(2)}) collective-permute-start(f32[1,3,256]{2,0,1:T(1,128)S(1)} %get-tuple-element.92), channel_id=1, source_target_pairs={{0,8},{8,16},{16,24},{24,0},{1,9},{9,17},{17,25},{25,1},{2,10},{10... | collective-permute-start | bytes 9224 | tf_op jit(solution)/shard_map/ppermute | solution.py:26
  458.4 9.8 %collective-permute-start.27 = (f32[1,3,256]{2,0,1:T(1,128)S(1)}, f32[1,3,256]{2,0,1:T(1,128)S(1)}, u32[]{:S(2)}, u32[]{:S(2)}) collective-permute-start(f32[1,3,256]{2,0,1:T(1,128)S(1)} %get-tuple-element.91), channel_id=1, source_target_pairs={{8,0},{16,8},{24,16},{0,24},{9,1},{17,9},{25,17},{1,25},{10,2},{18... | collective-permute-start | bytes 9224 | tf_op jit(solution)/shard_map/ppermute | solution.py:27
  464.3 16.3 %collective-permute-start.29 = (f32[1,3,256]{2,0,1:T(1,128)S(1)}, f32[1,3,256]{2,0,1:T(1,128)S(1)}, u32[]{:S(2)}, u32[]{:S(2)}) collective-permute-start(f32[1,3,256]{2,0,1:T(1,128)S(1)} %get-tuple-element.89), channel_id=1, source_target_pairs={{1,0},{2,1},{3,2},{4,3},{5,4},{6,5},{7,6},{0,7},{9,8},{10,9},{11,1... | collective-permute-start | bytes 9224 | tf_op jit(solution)/shard_map/ppermute | solution.py:27
  (24 other events, 268.1 us)
where the time goes:
time: 483 us; the launch traced here: 481 us
  other arithmetic  141 us (29%)
  starting transfers between devices  137 us (28%)
  local copies, waits for them, and re-layouts  121 us (25%)
  waiting for transfers between devices  80.3 us (17%)
    scatter-add x2, other arithmetic, per_device(): jax.ops.segment_sum(values, all_cells, num_segments=cells_extended)  122 us
    ppermute x15, starting transfers between devices, with_halo(): after = lax.ppermute(leading, axis, down)  89.5 us
    gather x4, local copies, waits for them, and re-layouts, per_device(): gathered = jnp.take(flat_results, all_cells, axis=1)  85 us
    ppermute x15, waiting for transfers between devices, with_halo(): after = lax.ppermute(leading, axis, down)  72.2 us
    ppermute x15, starting transfers between devices, with_halo(): before = lax.ppermute(last, axis, up)  47.7 us
  transfers between devices with their start and end apart: 30, of which 18 were waited for; matrix products, arithmetic and copies ran while one was open for 2% of the time, Pallas kernels for 0%

commit v1 on v0

v1 whole, which is shorter than its diff:
```python
import math

import jax
import jax.numpy as jnp
import numpy as np
from jax import lax
from jax.experimental import pallas as pl
from jax.experimental.pallas import tpu as pltpu
from jax.sharding import PartitionSpec as P

STEPS = 2
AXES = 64
CAP = 256
COSINE = math.cos(130.0 * math.pi / 180.0)
SINE = math.sin(130.0 * math.pi / 180.0)
GOLDEN = math.pi * (3.0 - math.sqrt(5.0))

LANES = 128
CHUNK = 1024
COLUMNS = 176
LAYERS = 18
WIDE = 256
MESH = pl.DeviceIdType.MESH
F32 = jnp.float32
BF16 = jnp.bfloat16
I32 = jnp.int32


def rotation_table():
    ordinal = np.arange(AXES) + 0.5
    height = 1.0 - 2.0 * ordinal / AXES
    radius = np.sqrt(1.0 - height * height)
    n = np.stack([radius * np.cos(ordinal * GOLDEN), radius * np.sin(ordinal * GOLDEN), height])
    zero = np.zeros(AXES)
    skew = np.array([[zero, -n[2], n[1]], [n[2], zero, -n[0]], [-n[1], n[0], zero]])
    matrix = COSINE * np.eye(3)[:, :, None] + SINE * skew + (1.0 - COSINE) * n[:, None] * n[None]
    table = np.zeros((3, 8, LANES), np.float32)
    for c in range(3):
        table[c, 0:3, :AXES] = matrix[:, c]
        table[c, 4:7, :AXES] = matrix[:, c]
    return table


def rows_of(shape):
    return lax.broadcasted_iota(I32, shape, 0)


def lanes_of(shape):
    return lax.broadcasted_iota(I32, shape, 1)


def cell_rows(coords, shift_ref, step):
    layer = []
    for d in range(3):
        shift = shift_ref[step, d]
        offset = jnp.where(shift > 0, 1, 0)
        layer.append(lax.shift_right_arithmetic(coords[d] - shift, 4) + offset)
    return column_of(layer[0], layer[1]), layer[2]


def column_of(first, second):
    inner = first * 32 + second
    return jnp.where(second == 32, first + 160, jnp.where(second == 0, first + 165, inner))


def one_hot(column):
    n = column.shape[1]
    rest = column.astype(F32) - rows_of((16, n)).astype(F32)
    rest = rest.astype(BF16)
    one, zero = jnp.ones((16, n), BF16), jnp.zeros((16, n), BF16)
    return jnp.concatenate(
        [jnp.where(rest == float(16 * j), one, zero) for j in range(COLUMNS // 16)], axis=0
    )


def deposit_rows(moving, weight, layer):
    n = moving.shape[1]
    row8 = rows_of((8, n))
    summand = moving * weight
    high = summand.astype(BF16).astype(F32)
    parts = jnp.where(row8 < 4, high, summand - high)
    parts = jnp.concatenate([parts, parts], axis=0).astype(BF16)
    half = lax.shift_right_logical(rows_of((16, n)), 3)
    rest = (layer - half).astype(F32).astype(BF16)
    zero = jnp.zeros((16, n), BF16)
    return jnp.concatenate(
        [jnp.where(rest == float(2 * j), parts, zero) for j in range(LAYERS // 2)], axis=0
    )


def collide(moving, layer, gathered, tables):
    n = moving.shape[1]
    chosen = gathered[0:8]
    for z in range(1, 17):
        chosen = jnp.where(layer == z, gathered[8 * z : 8 * z + 8], chosen)
    mean = chosen + pltpu.roll(chosen, 4, 0)
    axis = jnp.broadcast_to(mean[3:4], (8, n)).astype(I32)
    relative = moving - mean
    result = mean
    for c in range(3):
        columns = jnp.concatenate(
            [
                jnp.take_along_axis(tables[c], axis[:, i : i + LANES], axis=1)
                for i in range(0, n, LANES)
            ],
            axis=1,
        )
        result = result + columns * relative[c : c + 1]
    row8 = rows_of((8, n))
    return jnp.where((row8 & 3) == 3, 1.0, result)


def kernel(
    shift_ref, count_ref, velocity_ref, position_ref, bead_velocity_ref, bead_mass_ref,
    bead_position_ref, rot_ref, leave_ref, table_ref,
    velocity_out, bead_out, arrivals_out,
    moving, weight, cols, lays, onehots, totals, cells, results,
    send_y, send_x, recv_z, recv_y, recv_x,
    leave_table, leave_moving, leave_layer, leave_onehot, leave_send, leave_recv,
    send_sem, recv_sem,
):
    solvent = velocity_ref.shape[1]
    beads = bead_velocity_ref.shape[1]
    count = solvent + beads
    chunks = count // CHUNK

    names = ("gx", "gy", "gz")
    neighbour = []
    for name in names:
        size, me = lax.axis_size(name), lax.axis_index(name)
        neighbour.append((lax.rem(me + size - 1, size), lax.rem(me + 1, size)))

    barrier = pltpu.get_barrier_semaphore()
    for d in range(3):
        for side in range(2):
            pl.semaphore_signal(
                barrier, inc=1, device_id={names[d]: neighbour[d][side]}, device_id_type=MESH
            )

    def remote(src, dst, number, d, side):
        return pltpu.make_async_remote_copy(
            src_ref=src,
            dst_ref=dst,
            send_sem=send_sem.at[number],
            recv_sem=recv_sem.at[number],
            device_id={names[d]: neighbour[d][side]},
            device_id_type=MESH,
        )

    def load(velocity, where, length):
        moving[0:3, pl.ds(where, length)] = velocity
        moving[3:4, pl.ds(where, length)] = jnp.ones((1, length), F32)
        moving[4:7, pl.ds(where, length)] = velocity
        moving[7:8, pl.ds(where, length)] = jnp.ones((1, length), F32)

    load(velocity_ref[...], 0, solvent)
    load(bead_velocity_ref[...], solvent, beads)
    weight[:, 0:solvent] = jnp.ones((1, solvent), F32)
    weight[:, solvent:count] = bead_mass_ref[...]

    def place(step, first, number):
        def body(i, carry):
            here = pl.ds(pl.multiple_of(i * CHUNK, CHUNK), CHUNK)
            coords = [position_ref[d, step : step + 1, here] for d in range(3)]
            column, layer = cell_rows(coords, shift_ref, step)
            cols[step, :, here] = column
            lays[step, :, here] = layer
            onehots[step, :, here] = one_hot(column)
            return carry

        lax.fori_loop(first, first + number, body, 0)

    def place_beads(step):
        here = pl.ds(solvent, beads)
        coords = [bead_position_ref[d, step : step + 1, :] for d in range(3)]
        column, layer = cell_rows(coords, shift_ref, step)
        cols[step, :, here] = column
        lays[step, :, here] = layer
        onehots[step, :, here] = one_hot(column)

    def deposit(step, here, moved):
        rows = deposit_rows(moved, weight[:, here], lays[step, :, here])
        totals[...] += lax.dot_general(
            rows, onehots[step, :, here], (((1,), (1,)), ((), ())), preferred_element_type=F32
        )

    lane = lanes_of((8, LANES))

    def own_axes(step):
        offset = [jnp.where(shift_ref[step, d] > 0, 1, 0) for d in range(3)]
        local = rows_of((LANES, WIDE))
        target = column_of(
            lax.shift_right_logical(local, 5) + offset[0], (local & 31) + offset[1]
        )
        spread = jnp.where(lanes_of((LANES, WIDE)) == target, 1.0, 0.0).astype(BF16)
        held = jnp.concatenate([rot_ref[step, x] for x in range(4)], axis=1)
        by_layer = jnp.dot(
            held.astype(F32).astype(BF16), spread, preferred_element_type=F32
        )
        above = jnp.concatenate([jnp.zeros((1, WIDE), F32), by_layer], axis=0)
        below = jnp.concatenate([by_layer, jnp.zeros((1, WIDE), F32)], axis=0)
        return jnp.where(offset[2] > 0, above, below)

    def exchange(step, between):
        axes = own_axes(step)
        row8 = rows_of((8, WIDE))
        cells[:, :, COLUMNS:WIDE] = jnp.zeros((LAYERS, 8, WIDE - COLUMNS), F32)
        for z in range(17):
            part = totals[8 * z : 8 * z + 8, :]
            cells[z, :, 0:COLUMNS] = part + pltpu.roll(part, 4, 0)
            cells[z] = jnp.where(row8 == 7, axes[z : z + 1], cells[z])
        base = 6 * step
        if step == 0:
            pl.semaphore_wait(barrier, 6)

        low = remote(cells.at[0], recv_z.at[step, 1], base, 2, 0)
        high = remote(cells.at[16], recv_z.at[step, 0], base + 1, 2, 1)
        low.start()
        high.start()
        between(0)
        low.wait()
        high.wait()
        cells[0] += recv_z[step, 0]
        cells[16] += recv_z[step, 1]

        for group in range(2):
            packed = jnp.zeros((8, LANES), F32)
            for j in range(9):
                z = 9 * group + j
                if z < 17:
                    turned = pltpu.roll(cells[z, :, LANES:WIDE], (12 * j - 32) % LANES, 1)
                    packed = jnp.where((lane >= 12 * j) & (lane < 12 * j + 10), turned, packed)
            send_y[step, group] = packed
        low = remote(send_y.at[step], recv_y.at[step, 1], base + 2, 1, 0)
        high = remote(send_y.at[step], recv_y.at[step, 0], base + 3, 1, 1)
        low.start()
        high.start()
        between(1)
        low.wait()
        high.wait()
        place12 = lax.rem(lane, 12)
        for group in range(2):
            from_low = pltpu.roll(recv_y[step, 0, group], 5, 1)
            from_high = pltpu.roll(recv_y[step, 1, group], LANES - 5, 1)
            both = jnp.where(place12 < 5, from_high, from_low)
            for j in range(9):
                z = 9 * group + j
                if z < 17:
                    turned = pltpu.roll(both, (32 - 12 * j) % LANES, 1)
                    cells[z, :, LANES:WIDE] += jnp.where((lane >= 32) & (lane < 42), turned, 0.0)

        for group in range(6):
            packed_low = jnp.zeros((8, LANES), F32)
            packed_high = jnp.zeros((8, LANES), F32)
            for j in range(3):
                z = 3 * group + j
                if z < 17:
                    near, far = cells[z, :, 0:LANES], cells[z, :, LANES:WIDE]
                    face_low = jnp.where(lane < 32, near, far)
                    face_high = jnp.where(lane < 32, far, pltpu.roll(far, LANES - 4, 1))
                    if j:
                        face_low = pltpu.roll(face_low, 42 * j, 1)
                        face_high = pltpu.roll(face_high, 42 * j, 1)
                    inside = (lane >= 42 * j) & (lane < 42 * j + 38)
                    packed_low = jnp.where(inside, face_low, packed_low)
                    packed_high = jnp.where(inside, face_high, packed_high)
            send_x[step, 0, group] = packed_low
            send_x[step, 1, group] = packed_high
        low = remote(send_x.at[step, 0], recv_x.at[step, 1], base + 4, 0, 0)
        high = remote(send_x.at[step, 1], recv_x.at[step, 0], base + 5, 0, 1)
        low.start()
        high.start()
        between(2)
        low.wait()
        high.wait()
        ends = (lane == 32) | (lane == 37)
        ends_high = (lane == 36) | (lane == 41)
        row8 = rows_of((8, LANES))
        pending = None
        for group in range(6):
            for j in range(3):
                z = 3 * group + j
                if z < 17:
                    from_low, from_high = recv_x[step, 0, group], recv_x[step, 1, group]
                    if j:
                        from_low = pltpu.roll(from_low, LANES - 42 * j, 1)
                        from_high = pltpu.roll(from_high, LANES - 42 * j, 1)
                    near = cells[z, :, 0:LANES] + jnp.where(lane < 32, from_low, 0.0)
                    far = cells[z, :, LANES:WIDE] + jnp.where(
                        lane < 32,
                        from_high,
                        jnp.where(
                            ends,
                            from_low,
                            jnp.where(ends_high, pltpu.roll(from_high, 4, 1), 0.0),
                        ),
                    )
                    full = jnp.concatenate([near, far], axis=1)
                    row = rows_of((8, WIDE))
                    mean = full / jnp.maximum(full[3:4], 1.0)
                    rounded = mean.astype(BF16).astype(F32)
                    entry = jnp.where(row < 4, rounded, mean - rounded)
                    entry = jnp.where(row == 3, full[7:8], jnp.where(row == 7, 0.0, entry))
                else:
                    entry = jnp.zeros((8, WIDE), F32)
                if z % 2 == 0:
                    pending = entry
                else:
                    pair = jnp.concatenate([pending, entry], axis=0).astype(BF16)
                    results[8 * (z - 1) : 8 * (z + 1), :] = pair[:, 0:COLUMNS]

    tables = [table_ref[c] for c in range(3)]

    def gather_collide(step, here):
        gathered = jnp.dot(results[...], onehots[step, :, here], preferred_element_type=F32)
        return collide(moving[:, here], lays[step, :, here], gathered, tables)

    solvent_chunks = solvent // CHUNK
    totals[...] = jnp.zeros_like(totals)
    place(0, 0, solvent_chunks)
    place_beads(0)

    def first_deposit(i, carry):
        here = pl.ds(pl.multiple_of(i * CHUNK, CHUNK), CHUNK)
        deposit(0, here, moving[:, here])
        return carry

    lax.fori_loop(0, chunks, first_deposit, 0)

    def between_first(number):
        if number == 0:
            place(1, 0, 4)
        elif number == 1:
            place(1, 4, 4)
        else:
            place(1, 8, solvent_chunks - 8)
            place_beads(1)

    exchange(0, between_first)

    totals[...] = jnp.zeros_like(totals)

    def turn(i, carry):
        here = pl.ds(pl.multiple_of(i * CHUNK, CHUNK), CHUNK)
        moved = gather_collide(0, here)
        moving[:, here] = moved
        deposit(1, here, moved)
        return carry

    lax.fori_loop(0, chunks, turn, 0)

    tiles = solvent // LANES

    def between_second(number):
        if number == 0:
            row8 = rows_of((8, LANES))

            def body(i, carry):
                parts = []
                for k in range(2):
                    here = pl.ds(pl.multiple_of((2 * i + k) * LANES, LANES), LANES)
                    now = moving[:, here]
                    rounded = now.astype(BF16).astype(F32)
                    entry = jnp.where(row8 < 4, rounded, now - rounded)
                    entry = jnp.where(row8 == 3, cols[1, :, here].astype(F32), entry)
                    parts.append(jnp.where(row8 == 7, lays[1, :, here].astype(F32), entry))
                leave_table[pl.ds(pl.multiple_of(16 * i, 16), 16), :] = jnp.concatenate(
                    parts, axis=0
                ).astype(BF16)
                return carry

            lax.fori_loop(0, tiles // 2, body, 0)
        elif number == 1:

            def body(d, carry):
                for side in range(2):
                    index = jnp.maximum(leave_ref[d, side : side + 1, :], 0)
                    offset = (index & (LANES - 1)).astype(F32)
                    rest = (offset - rows_of((16, CAP)).astype(F32)).astype(BF16)
                    one, zero = jnp.ones((16, CAP), BF16), jnp.zeros((16, CAP), BF16)
                    spot = jnp.concatenate(
                        [jnp.where(rest == float(16 * j), one, zero) for j in range(8)], axis=0
                    )
                    found = jnp.dot(leave_table[...], spot, preferred_element_type=F32)
                    tile = lax.shift_right_logical(index, 7)
                    chosen = found[0:8]
                    for i in range(1, tiles):
                        chosen = jnp.where(tile == i, found[8 * i : 8 * i + 8], chosen)
                    leave_moving[d, side] = chosen + pltpu.roll(chosen, 4, 0)
                    leave_layer[d, side] = chosen[7:8].astype(I32)
                    leave_onehot[d, side] = one_hot(chosen[3:4].astype(I32))
                return carry

            lax.fori_loop(0, 3, body, 0)

    exchange(1, between_second)

    slot = lanes_of((8, CAP))
    travels = []
    for d in range(3):
        for side in range(2):
            gathered = jnp.dot(
                results[...], leave_onehot[d, side], preferred_element_type=F32
            )
            moved = collide(leave_moving[d, side], leave_layer[d, side], gathered, tables)
            leave_send[d, side] = jnp.where(slot < count_ref[side, d], moved, 0.0)
            travel = remote(
                leave_send.at[d, side], leave_recv.at[d, 1 - side], 12 + 2 * d + side, d, side
            )
            travel.start()
            travels.append(travel)

    def finish(i, carry):
        here = pl.ds(pl.multiple_of(i * CHUNK, CHUNK), CHUNK)
        velocity_out[:, here] = gather_collide(1, here)[0:3]
        return carry

    lax.fori_loop(0, solvent_chunks, finish, 0)
    bead_out[...] = gather_collide(1, pl.ds(solvent, beads))[0:3]

    for travel in travels:
        travel.wait()
    for d in range(3):
        for side in range(2):
            arrivals_out[d, :, side, :] = leave_recv[d, side, 0:3, :]


def per_device(
    velocity, position, bead_velocity, bead_mass, bead_position, grid_shift, rot_axis,
    leave_count, leave_index,
):
    solvent, beads = velocity.shape[1], bead_velocity.shape[1]
    count = solvent + beads
    vmem = pl.BlockSpec(memory_space=pltpu.VMEM)
    smem = pl.BlockSpec(memory_space=pltpu.SMEM)
    velocity_out, bead_out, arrivals = pl.pallas_call(
        kernel,
        out_shape=(
            jax.ShapeDtypeStruct((3, solvent), F32),
            jax.ShapeDtypeStruct((3, beads), F32),
            jax.ShapeDtypeStruct((3, 3, 2, CAP), F32),
        ),
        in_specs=[smem, smem] + [vmem] * 8,
        out_specs=(vmem, vmem, vmem),
        scratch_shapes=[
            pltpu.VMEM((8, count), F32),
            pltpu.VMEM((1, count), F32),
            pltpu.VMEM((2, 1, count), I32),
            pltpu.VMEM((2, 1, count), I32),
            pltpu.VMEM((2, COLUMNS, count), BF16),
            pltpu.VMEM((8 * LAYERS, COLUMNS), F32),
            pltpu.VMEM((LAYERS, 8, WIDE), F32),
            pltpu.VMEM((8 * LAYERS, COLUMNS), BF16),
            pltpu.VMEM((2, 2, 8, LANES), F32),
            pltpu.VMEM((2, 2, 6, 8, LANES), F32),
            pltpu.VMEM((2, 2, 8, WIDE), F32),
            pltpu.VMEM((2, 2, 2, 8, LANES), F32),
            pltpu.VMEM((2, 2, 6, 8, LANES), F32),
            pltpu.VMEM((8 * solvent // LANES, LANES), BF16),
            pltpu.VMEM((3, 2, 8, CAP), F32),
            pltpu.VMEM((3, 2, 1, CAP), I32),
            pltpu.VMEM((3, 2, COLUMNS, CAP), BF16),
            pltpu.VMEM((3, 2, 8, CAP), F32),
            pltpu.VMEM((3, 2, 8, CAP), F32),
            pltpu.SemaphoreType.DMA((18,)),
            pltpu.SemaphoreType.DMA((18,)),
        ],
        compiler_params=pltpu.CompilerParams(
            collective_id=0, has_side_effects=True, vmem_limit_bytes=40 * 1024 * 1024
        ),
        cost_estimate=pl.CostEstimate(flops=10**9, bytes_accessed=10**6, transcendentals=0),
        name="collisions",
    )(
        grid_shift,
        leave_count.reshape(3, 2).T,
        velocity,
        jnp.transpose(position, (1, 0, 2)),
        bead_velocity,
        bead_mass.reshape(1, beads),
        jnp.transpose(bead_position, (1, 0, 2)),
        jnp.swapaxes(rot_axis, 2, 3),
        leave_index,
        jnp.asarray(rotation_table()),
    )
    return velocity_out, bead_out, jnp.transpose(arrivals, (0, 2, 1, 3))


def solution(mesh):
    return jax.shard_map(
        per_device,
        mesh=mesh,
        in_specs=(
            P(None, ("gx", "gy", "gz")),
            P(None, None, ("gx", "gy", "gz")),
            P(None, ("gx", "gy", "gz")),
            P(("gx", "gy", "gz")),
            P(None, None, ("gx", "gy", "gz")),
            P(),
            P(None, "gx", "gy", "gz"),
            P(None, None, ("gx", "gy", "gz")),
            P(None, None, ("gx", "gy", "gz")),
        ),
        out_specs=(
            P(None, ("gx", "gy", "gz")),
            P(None, ("gx", "gy", "gz")),
            P(None, None, None, ("gx", "gy", "gz")),
        ),
        check_vma=False,
    )
```

time: 483 us -> 73.9 us (0.15)
  the two profiles are of different devices: /device:TPU:24 before, /device:TPU:2 now
where the time goes in v1:
time: 73.9 us; the launch traced here: 73.4 us
  Pallas kernels  64.7 us (88%)
  local copies, waits for them, and re-layouts  8.11 us (11%)
    pallas_call x1, Pallas kernels, per_device(): pl.pallas_call(kernel, out_shape=(jax.ShapeDtypeStruct((3, solvent), F32)...  64.7 us
    unnamed x23, local copies, waits for them, and re-layouts  8.11 us

profile of v1, /device:TPU:2, one launch (start us, length us, event | category | flops | bytes accessed | tf_op | source)
XLA Modules:
  0.0 73.4 jit_solution(13327180819382349157)
XLA Ops:
  0.6 0.0 copy-start.5
  0.6 0.0 copy-start.8
  0.7 0.0 copy-start.7
  0.7 0.7 copy-done.5
  1.3 0.0 copy-done.8
  1.3 0.0 copy-done.7
  1.3 0.0 copy-start
  1.3 0.9 %copy-done = s32[2,3,10240]{2,0,1:T(2,128)S(1)} copy-done((s32[2,3,10240]{2,0,1:T(2,128)S(1)}, s32[2,3,10240]{2,0,1:T(2,128)}, u32[]{:S(2)}) %copy-start) | copy-done | bytes 245784
  2.3 0.0 copy-start.1
  2.3 0.9 %copy-done.1 = f32[3,10240]{1,0:T(4,128)S(1)} copy-done((f32[3,10240]{1,0:T(4,128)S(1)}, f32[3,10240]{1,0:T(4,128)}, u32[]{:S(2)}) %copy-start.1) | copy-done | bytes 122904
  3.2 0.0 copy-start.2
  3.2 0.8 %copy-done.2 = s32[2,4,32,16]{2,3,1,0:T(8,128)S(1)} copy-done((s32[2,4,32,16]{2,3,1,0:T(8,128)S(1)}, s32[2,4,32,16]{2,3,1,0:T(8,128)}, u32[]{:S(2)}) %copy-start.2) | copy-done | bytes 16408
  4.0 0.0 copy-start.3
  4.0 0.7 %copy-done.3 = s32[2,3,1024]{2,0,1:T(2,128)S(1)} copy-done((s32[2,3,1024]{2,0,1:T(2,128)S(1)}, s32[2,3,1024]{2,0,1:T(2,128)}, u32[]{:S(2)}) %copy-start.3) | copy-done | bytes 24600
  4.8 0.0 copy-start.4
  4.8 0.7 copy-done.4
  5.5 0.0 copy-start.6
  5.5 0.7 copy-done.6
  6.2 0.0 copy-start.9
  6.2 0.7 copy-done.9
  6.9 64.7 %collisions.1 = (f32[3,10240]{1,0:T(4,128)S(1)}, f32[3,1024]{1,0:T(4,128)S(1)}, f32[3,3,2,256]{3,2,1,0:T(2,128)S(1)}) custom-call(s32[2,3]{1,0:T(2,128)S(1)} %copy-done.7, s32[2,3]{1,0:T(2,128)S(1)} %bitcast.13, f32[3,10240]{1,0:T(4,128)S(1)} %copy-done.1, s32[3,2,10240]{2,1,0:T(2,128)S(1)} %bitcast.9, f32[3,1024]{1,0:T(4,128)S(1)} %copy-done.4, ...), custom_call_target="tpu_custom_call" | custom-call | flops 1000000000 | bytes 1000000 | tf_op jit(solution)/shard_map/collisions/pallas_call | solution.py:436
  71.6 0.7 copy.16
  72.2 0.6 copy.17
  72.8 0.6 copy.18
Async XLA Ops:
  0.6 0.7 copy-start.5
  0.6 0.7 copy-start.8
  0.7 0.7 copy-start.7
  1.3 0.9 %copy-start = (s32[2,3,10240]{2,0,1:T(2,128)S(1)}, s32[2,3,10240]{2,0,1:T(2,128)}, u32[]{:S(2)}) copy-start(s32[2,3,10240]{2,0,1:T(2,128)} %param.11) | copy-start | bytes 737284
  2.3 0.9 %copy-start.1 = (f32[3,10240]{1,0:T(4,128)S(1)}, f32[3,10240]{1,0:T(4,128)}, u32[]{:S(2)}) copy-start(f32[3,10240]{1,0:T(4,128)} %velocity_ref.1) | copy-start | bytes 368644
  3.2 0.8 %copy-start.2 = (s32[2,4,32,16]{2,3,1,0:T(8,128)S(1)}, s32[2,4,32,16]{2,3,1,0:T(8,128)}, u32[]{:S(2)}) copy-start(s32[2,4,32,16]{2,3,1,0:T(8,128)} %param.16) | copy-start | bytes 49156
  4.0 0.7 %copy-start.3 = (s32[2,3,1024]{2,0,1:T(2,128)S(1)}, s32[2,3,1024]{2,0,1:T(2,128)}, u32[]{:S(2)}) copy-start(s32[2,3,1024]{2,0,1:T(2,128)} %param.14) | copy-start | bytes 73732
  4.8 0.7 copy-start.4
  5.5 0.7 copy-start.6
  6.2 0.7 copy-start.9

commit v2 on v1

--- a/solution.py
+++ b/solution.py
@@ -41,12 +41,37 @@
     return table
 
 
+OFFSETS = [
+    (dx, dy, dz)
+    for dx in (-1, 0, 1)
+    for dy in (-1, 0, 1)
+    for dz in (-1, 0, 1)
+    if (dx, dy, dz) != (0, 0, 0)
+]
+EDGES = [(dx, dy) for dx in (-1, 0, 1) for dy in (-1, 1)]
+
+
+def moved_edge(edge, place):
+    dx, dy = edge
+    target = {1: 0, -1: 5}[dy] + (4 if dx == 1 else 0)
+    source = {1: 5, -1: 0}[dy] + (4 if dx == -1 else 0)
+    if dx == 0:
+        chosen = (place >= target) & (place < target + 5)
+    else:
+        chosen = place == target
+    return (target - source) % LANES, chosen
+
+
 def rows_of(shape):
     return lax.broadcasted_iota(I32, shape, 0)
 
 
 def lanes_of(shape):
     return lax.broadcasted_iota(I32, shape, 1)
+
+
+def lanes_from(tile, source):
+    return jnp.take_along_axis(tile, source & (LANES - 1), axis=1)
 
 
 def cell_rows(coords, shift_ref, step):
@@ -111,11 +136,13 @@
 
 
 def kernel(
+    shift_hbm, count_hbm, velocity_hbm, position_hbm, bead_velocity_hbm, bead_mass_hbm,
+    bead_position_hbm, rot_hbm, leave_hbm, table_hbm,
+    velocity_out, bead_out, arrivals_out,
     shift_ref, count_ref, velocity_ref, position_ref, bead_velocity_ref, bead_mass_ref,
-    bead_position_ref, rot_ref, leave_ref, table_ref,
-    velocity_out, bead_out, arrivals_out,
+    bead_position_ref, rot_ref, leave_ref, table_ref, load_sem,
     moving, weight, cols, lays, onehots, totals, cells, results,
-    send_y, send_x, recv_z, recv_y, recv_x,
+    send_z, send_y, send_x, recv_edge, recv_line, recv_z, recv_y, recv_x,
     leave_table, leave_moving, leave_layer, leave_onehot, leave_send, leave_recv,
     send_sem, recv_sem,
 ):
@@ -125,25 +152,48 @@
     chunks = count // CHUNK
 
     names = ("gx", "gy", "gz")
-    neighbour = []
-    for name in names:
-        size, me = lax.axis_size(name), lax.axis_index(name)
-        neighbour.append((lax.rem(me + size - 1, size), lax.rem(me + 1, size)))
+
+    def device_at(offset):
+        where = {}
+        for name, step_by in zip(names, offset):
+            if step_by:
+                size, me = lax.axis_size(name), lax.axis_index(name)
+                where[name] = lax.rem(me + size + step_by, size)
+        return where
 
     barrier = pltpu.get_barrier_semaphore()
-    for d in range(3):
-        for side in range(2):
-            pl.semaphore_signal(
-                barrier, inc=1, device_id={names[d]: neighbour[d][side]}, device_id_type=MESH
+    for offset in OFFSETS:
+        pl.semaphore_signal(barrier, inc=1, device_id=device_at(offset), device_id_type=MESH)
+
+    loads = [
+        pltpu.make_async_copy(src, dst, load_sem.at[i])
+        for i, (src, dst) in enumerate(
+            (
+                (shift_hbm, shift_ref),
+                (position_hbm, position_ref),
+                (bead_position_hbm, bead_position_ref),
+                (velocity_hbm, velocity_ref),
+                (bead_velocity_hbm, bead_velocity_ref),
+                (bead_mass_hbm, bead_mass_ref),
+                (rot_hbm, rot_ref),
+                (leave_hbm, leave_ref),
+                (count_hbm, count_ref),
+                (table_hbm, table_ref),
             )
-
-    def remote(src, dst, number, d, side):
+        )
+    ]
+    for copy in loads:
+        copy.start()
+    for copy in loads:
+        copy.wait()
+
+    def remote(src, dst, number, offset):
         return pltpu.make_async_remote_copy(
             src_ref=src,
             dst_ref=dst,
             send_sem=send_sem.at[number],
             recv_sem=recv_sem.at[number],
-            device_id={names[d]: neighbour[d][side]},
+            device_id=device_at(offset),
             device_id_type=MESH,
         )
 
@@ -203,26 +253,62 @@
 
     def exchange(step, between):
         axes = own_axes(step)
-        row8 = rows_of((8, WIDE))
+        row8w = rows_of((8, WIDE))
+        row8 = rows_of((8, LANES))
         cells[:, :, COLUMNS:WIDE] = jnp.zeros((LAYERS, 8, WIDE - COLUMNS), F32)
-        for z in range(17):
+
+        def settle(z):
             part = totals[8 * z : 8 * z + 8, :]
             cells[z, :, 0:COLUMNS] = part + pltpu.roll(part, 4, 0)
-            cells[z] = jnp.where(row8 == 7, axes[z : z + 1], cells[z])
-        base = 6 * step
+            cells[z] = jnp.where(row8w == 7, axes[z : z + 1], cells[z])
+
+        settle(0)
+        settle(16)
+        for side in range(2):
+            near, far = cells[16 * side, :, 0:LANES], cells[16 * side, :, LANES:WIDE]
+            edge = lanes_from(far, lane + 32 - 10 * row8)
+            edge = jnp.where((lane >= 10 * row8) & (lane < 10 * row8 + 10), edge, 0.0)
+            send_z[step, side, 2:3] = jnp.sum(edge, axis=0, keepdims=True)
+            for at, tile in ((0, near), (3, far)):
+                line = lanes_from(tile, lane & 31)
+                line = jnp.where(lax.shift_right_logical(lane, 5) == (row8 & 3), line, 0.0)
+                for half in range(2):
+                    send_z[step, side, at + half : at + half + 1] = jnp.sum(
+                        line[4 * half : 4 * half + 4], axis=0, keepdims=True
+                    )
+            send_z[step, side, 5:9] = near[0:4]
+            send_z[step, side, 9:10] = near[7:8]
+
         if step == 0:
-            pl.semaphore_wait(barrier, 6)
-
-        low = remote(cells.at[0], recv_z.at[step, 1], base, 2, 0)
-        high = remote(cells.at[16], recv_z.at[step, 0], base + 1, 2, 1)
-        low.start()
-        high.start()
-        between(0)
-        low.wait()
-        high.wait()
-        cells[0] += recv_z[step, 0]
-        cells[16] += recv_z[step, 1]
-
+            pl.semaphore_wait(barrier, len(OFFSETS))
+
+        travels = {}
+
+        def send(src, dst, offset):
+            travel = remote(src, dst, len(OFFSETS) * step + OFFSETS.index(offset), offset)
+            travel.start()
+            travels[offset] = travel
+
+        for side in range(2):
+            dz = 2 * side - 1
+            for dx in (-1, 0, 1):
+                for dy in (-1, 1):
+                    back = EDGES.index((-dx, -dy))
+                    send(
+                        send_z.at[step, side, pl.ds(2, 1)],
+                        recv_edge.at[step, 1 - side, back],
+                        (dx, dy, dz),
+                    )
+            for dx in (-1, 1):
+                send(
+                    send_z.at[step, side, pl.ds(1 + dx, 3)],
+                    recv_line.at[step, 1 - side, (1 - dx) // 2],
+                    (dx, 0, dz),
+                )
+            send(send_z.at[step, side, pl.ds(2, 8)], recv_z.at[step, 1 - side], (0, 0, dz))
+
+        for z in range(1, 16):
+            settle(z)
         for group in range(2):
             packed = jnp.zeros((8, LANES), F32)
             for j in range(9):
@@ -231,23 +317,10 @@
                     turned = pltpu.roll(cells[z, :, LANES:WIDE], (12 * j - 32) % LANES, 1)
                     packed = jnp.where((lane >= 12 * j) & (lane < 12 * j + 10), turned, packed)
             send_y[step, group] = packed
-        low = remote(send_y.at[step], recv_y.at[step, 1], base + 2, 1, 0)
-        high = remote(send_y.at[step], recv_y.at[step, 0], base + 3, 1, 1)
-        low.start()
-        high.start()
-        between(1)
-        low.wait()
-        high.wait()
-        place12 = lax.rem(lane, 12)
-        for group in range(2):
-            from_low = pltpu.roll(recv_y[step, 0, group], 5, 1)
-            from_high = pltpu.roll(recv_y[step, 1, group], LANES - 5, 1)
-            both = jnp.where(place12 < 5, from_high, from_low)
-            for j in range(9):
-                z = 9 * group + j
-                if z < 17:
-                    turned = pltpu.roll(both, (32 - 12 * j) % LANES, 1)
-                    cells[z, :, LANES:WIDE] += jnp.where((lane >= 32) & (lane < 42), turned, 0.0)
+        for dx in (-1, 0, 1):
+            for dy in (-1, 1):
+                back = EDGES.index((-dx, -dy))
+                send(send_y.at[step], recv_y.at[step, back], (dx, dy, 0))
 
         for group in range(6):
             packed_low = jnp.zeros((8, LANES), F32)
@@ -266,17 +339,24 @@
                     packed_high = jnp.where(inside, face_high, packed_high)
             send_x[step, 0, group] = packed_low
             send_x[step, 1, group] = packed_high
-        low = remote(send_x.at[step, 0], recv_x.at[step, 1], base + 4, 0, 0)
-        high = remote(send_x.at[step, 1], recv_x.at[step, 0], base + 5, 0, 1)
-        low.start()
-        high.start()
-        between(2)
-        low.wait()
-        high.wait()
+        send(send_x.at[step, 0], recv_x.at[step, 1], (-1, 0, 0))
+        send(send_x.at[step, 1], recv_x.at[step, 0], (1, 0, 0))
+
+        between()
+
+        for offset, travel in travels.items():
+            if offset[2] == 0:
+                travel.wait()
+        place12 = lax.rem(lane, 12)
+        both_groups = []
+        for group in range(2):
+            both = jnp.zeros((8, LANES), F32)
+            for k, edge in enumerate(EDGES):
+                turn_by, chosen = moved_edge(edge, place12)
+                both += jnp.where(chosen, pltpu.roll(recv_y[step, k, group], turn_by, 1), 0.0)
+            both_groups.append(both)
         ends = (lane == 32) | (lane == 37)
         ends_high = (lane == 36) | (lane == 41)
-        row8 = rows_of((8, LANES))
-        pending = None
         for group in range(6):
             for j in range(3):
                 z = 3 * group + j
@@ -285,29 +365,65 @@
                     if j:
                         from_low = pltpu.roll(from_low, LANES - 42 * j, 1)
                         from_high = pltpu.roll(from_high, LANES - 42 * j, 1)
-                    near = cells[z, :, 0:LANES] + jnp.where(lane < 32, from_low, 0.0)
-                    far = cells[z, :, LANES:WIDE] + jnp.where(
-                        lane < 32,
-                        from_high,
+                    shift_by = (32 - 12 * (z % 9)) % LANES
+                    from_second = pltpu.roll(both_groups[z // 9], shift_by, 1)
+                    cells[z, :, 0:LANES] += jnp.where(lane < 32, from_low, 0.0)
+                    cells[z, :, LANES:WIDE] += (
                         jnp.where(
-                            ends,
-                            from_low,
-                            jnp.where(ends_high, pltpu.roll(from_high, 4, 1), 0.0),
-                        ),
+                            lane < 32,
+                            from_high,
+                            jnp.where(
+                                ends,
+                                from_low,
+                                jnp.where(ends_high, pltpu.roll(from_high, 4, 1), 0.0),
+                            ),
+                        )
+                        + jnp.where((lane >= 32) & (lane < 42), from_second, 0.0)
                     )
-                    full = jnp.concatenate([near, far], axis=1)
-                    row = rows_of((8, WIDE))
-                    mean = full / jnp.maximum(full[3:4], 1.0)
-                    rounded = mean.astype(BF16).astype(F32)
-                    entry = jnp.where(row < 4, rounded, mean - rounded)
-                    entry = jnp.where(row == 3, full[7:8], jnp.where(row == 7, 0.0, entry))
-                else:
-                    entry = jnp.zeros((8, WIDE), F32)
-                if z % 2 == 0:
-                    pending = entry
-                else:
-                    pair = jnp.concatenate([pending, entry], axis=0).astype(BF16)
-                    results[8 * (z - 1) : 8 * (z + 1), :] = pair[:, 0:COLUMNS]
+
+        def entry_of(z):
+            if z == 17:
+                return jnp.zeros((8, WIDE), F32)
+            full = cells[z]
+            full = jnp.where((row8w >= 4) & (row8w < 7), pltpu.roll(full, 4, 0), full)
+            mean = full / jnp.maximum(full[3:4], 1.0)
+            rounded = mean.astype(BF16).astype(F32)
+            entry = jnp.where(row8w < 4, rounded, mean - rounded)
+            return jnp.where(row8w == 3, full[7:8], jnp.where(row8w == 7, 0.0, entry))
+
+        def finish_pair(z):
+            pair = jnp.concatenate([entry_of(z), entry_of(z + 1)], axis=0).astype(BF16)
+            results[8 * z : 8 * z + 16, :] = pair[:, 0:COLUMNS]
+
+        for z in range(2, 16, 2):
+            finish_pair(z)
+
+        for offset, travel in travels.items():
+            if offset[2] != 0:
+                travel.wait()
+        for side in range(2):
+            face = recv_z[step, side]
+            lane1 = lanes_of((1, LANES))
+            place10 = lax.rem(lane1, 10)
+            edge = face[0:1]
+            for k, offset in enumerate(EDGES):
+                turn_by, chosen = moved_edge(offset, place10)
+                edge += jnp.where(chosen, pltpu.roll(recv_edge[step, side, k], turn_by, 1), 0.0)
+            low, high = recv_line[step, side, 0], recv_line[step, side, 1]
+            at_low, at_high = (place10 == 0) | (place10 == 5), (place10 == 4) | (place10 == 9)
+            edge += jnp.where(at_low, pltpu.roll(low[0:1], LANES - 4, 1), 0.0)
+            edge += jnp.where(at_high, pltpu.roll(high[2:3], 4, 1), 0.0)
+            edge = lanes_from(jnp.broadcast_to(edge, (8, LANES)), lane - 32 + 10 * row8)
+            lines = []
+            for line in (low[1:3], face[1:3] + high[0:2]):
+                wide = jnp.where(row8 < 4, line[0:1], line[1:2])
+                lines.append(lanes_from(wide, (lane & 31) + 32 * (row8 & 3)))
+            rest = jnp.where(row8 == 7, face, pltpu.roll(face, 5, 0))
+            near = rest + jnp.where(lane < 32, lines[0], 0.0)
+            far = jnp.where(lane < 32, lines[1], jnp.where(lane < 42, edge, 0.0))
+            cells[16 * side, :, 0:LANES] += near
+            cells[16 * side, :, LANES:WIDE] += far
+            finish_pair(16 * side)
 
     tables = [table_ref[c] for c in range(3)]
 
@@ -327,14 +443,9 @@
 
     lax.fori_loop(0, chunks, first_deposit, 0)
 
-    def between_first(number):
-        if number == 0:
-            place(1, 0, 4)
-        elif number == 1:
-            place(1, 4, 4)
-        else:
-            place(1, 8, solvent_chunks - 8)
-            place_beads(1)
+    def between_first():
+        place(1, 0, solvent_chunks)
+        place_beads(1)
 
     exchange(0, between_first)
 
@@ -351,47 +462,45 @@
 
     tiles = solvent // LANES
 
-    def between_second(number):
-        if number == 0:
-            row8 = rows_of((8, LANES))
-
-            def body(i, carry):
-                parts = []
-                for k in range(2):
-                    here = pl.ds(pl.multiple_of((2 * i + k) * LANES, LANES), LANES)
-                    now = moving[:, here]
-                    rounded = now.astype(BF16).astype(F32)
-                    entry = jnp.where(row8 < 4, rounded, now - rounded)
-                    entry = jnp.where(row8 == 3, cols[1, :, here].astype(F32), entry)
-                    parts.append(jnp.where(row8 == 7, lays[1, :, here].astype(F32), entry))
-                leave_table[pl.ds(pl.multiple_of(16 * i, 16), 16), :] = jnp.concatenate(
-                    parts, axis=0
-                ).astype(BF16)
-                return carry
-
-            lax.fori_loop(0, tiles // 2, body, 0)
-        elif number == 1:
-
-            def body(d, carry):
-                for side in range(2):
-                    index = jnp.maximum(leave_ref[d, side : side + 1, :], 0)
-                    offset = (index & (LANES - 1)).astype(F32)
-                    rest = (offset - rows_of((16, CAP)).astype(F32)).astype(BF16)
-                    one, zero = jnp.ones((16, CAP), BF16), jnp.zeros((16, CAP), BF16)
-                    spot = jnp.concatenate(
-                        [jnp.where(rest == float(16 * j), one, zero) for j in range(8)], axis=0
-                    )
-                    found = jnp.dot(leave_table[...], spot, preferred_element_type=F32)
-                    tile = lax.shift_right_logical(index, 7)
-                    chosen = found[0:8]
-                    for i in range(1, tiles):
-                        chosen = jnp.where(tile == i, found[8 * i : 8 * i + 8], chosen)
-                    leave_moving[d, side] = chosen + pltpu.roll(chosen, 4, 0)
-                    leave_layer[d, side] = chosen[7:8].astype(I32)
-                    leave_onehot[d, side] = one_hot(chosen[3:4].astype(I32))
-                return carry
-
-            lax.fori_loop(0, 3, body, 0)
+    def between_second():
+        row8 = rows_of((8, LANES))
+
+        def fill(i, carry):
+            parts = []
+            for k in range(2):
+                here = pl.ds(pl.multiple_of((2 * i + k) * LANES, LANES), LANES)
+                now = moving[:, here]
+                rounded = now.astype(BF16).astype(F32)
+                entry = jnp.where(row8 < 4, rounded, now - rounded)
+                entry = jnp.where(row8 == 3, cols[1, :, here].astype(F32), entry)
+                parts.append(jnp.where(row8 == 7, lays[1, :, here].astype(F32), entry))
+            leave_table[pl.ds(pl.multiple_of(16 * i, 16), 16), :] = jnp.concatenate(
+                parts, axis=0
+            ).astype(BF16)
+            return carry
+
+        lax.fori_loop(0, tiles // 2, fill, 0)
+
+        def pick(d, carry):
+            for side in range(2):
+                index = jnp.maximum(leave_ref[d, side : side + 1, :], 0)
+                offset = (index & (LANES - 1)).astype(F32)
+                rest = (offset - rows_of((16, CAP)).astype(F32)).astype(BF16)
+                one, zero = jnp.ones((16, CAP), BF16), jnp.zeros((16, CAP), BF16)
+                spot = jnp.concatenate(
+                    [jnp.where(rest == float(16 * j), one, zero) for j in range(8)], axis=0
+                )
+                found = jnp.dot(leave_table[...], spot, preferred_element_type=F32)
+                tile = lax.shift_right_logical(index, 7)
+                chosen = found[0:8]
+                for i in range(1, tiles):
+                    chosen = jnp.where(tile == i, found[8 * i : 8 * i + 8], chosen)
+                leave_moving[d, side] = chosen + pltpu.roll(chosen, 4, 0)
+                leave_layer[d, side] = chosen[7:8].astype(I32)
+                leave_onehot[d, side] = one_hot(chosen[3:4].astype(I32))
+            return carry
+
+        lax.fori_loop(0, 3, pick, 0)
 
     exchange(1, between_second)
 
@@ -404,8 +513,12 @@
             )
             moved = collide(leave_moving[d, side], leave_layer[d, side], gathered, tables)
             leave_send[d, side] = jnp.where(slot < count_ref[side, d], moved, 0.0)
+            offset = tuple(2 * side - 1 if axis == d else 0 for axis in range(3))
             travel = remote(
-                leave_send.at[d, side], leave_recv.at[d, 1 - side], 12 + 2 * d + side, d, side
+                leave_send.at[d, side],
+                leave_recv.at[d, 1 - side],
+                2 * len(OFFSETS) + 2 * d + side,
+                offset,
             )
             travel.start()
             travels.append(travel)
@@ -432,7 +545,6 @@
     solvent, beads = velocity.shape[1], bead_velocity.shape[1]
     count = solvent + beads
     vmem = pl.BlockSpec(memory_space=pltpu.VMEM)
-    smem = pl.BlockSpec(memory_space=pltpu.SMEM)
     velocity_out, bead_out, arrivals = pl.pallas_call(
         kernel,
         out_shape=(
@@ -440,9 +552,20 @@
             jax.ShapeDtypeStruct((3, beads), F32),
             jax.ShapeDtypeStruct((3, 3, 2, CAP), F32),
         ),
-        in_specs=[smem, smem] + [vmem] * 8,
+        in_specs=[pl.BlockSpec(memory_space=pltpu.HBM)] * 10,
         out_specs=(vmem, vmem, vmem),
         scratch_shapes=[
+            pltpu.SMEM((2, 3), I32),
+            pltpu.SMEM((2, 3), I32),
+            pltpu.VMEM((3, solvent), F32),
+            pltpu.VMEM((3, 2, solvent), I32),
+            pltpu.VMEM((3, beads), F32),
+            pltpu.VMEM((1, beads), F32),
+            pltpu.VMEM((3, 2, beads), I32),
+            pltpu.VMEM((2, 4, 16, 32), I32),
+            pltpu.VMEM((3, 2, CAP), I32),
+            pltpu.VMEM((3, 8, LANES), F32),
+            pltpu.SemaphoreType.DMA((10,)),
             pltpu.VMEM((8, count), F32),
             pltpu.VMEM((1, count), F32),
             pltpu.VMEM((2, 1, count), I32),
@@ -451,10 +574,13 @@
             pltpu.VMEM((8 * LAYERS, COLUMNS), F32),
             pltpu.VMEM((LAYERS, 8, WIDE), F32),
             pltpu.VMEM((8 * LAYERS, COLUMNS), BF16),
+            pltpu.VMEM((2, 2, 16, LANES), F32),
             pltpu.VMEM((2, 2, 8, LANES), F32),
             pltpu.VMEM((2, 2, 6, 8, LANES), F32),
-            pltpu.VMEM((2, 2, 8, WIDE), F32),
-            pltpu.VMEM((2, 2, 2, 8, LANES), F32),
+            pltpu.VMEM((2, 2, 6, 1, LANES), F32),
+            pltpu.VMEM((2, 2, 2, 3, LANES), F32),
+            pltpu.VMEM((2, 2, 8, LANES), F32),
+            pltpu.VMEM((2, 6, 2, 8, LANES), F32),
             pltpu.VMEM((2, 2, 6, 8, LANES), F32),
             pltpu.VMEM((8 * solvent // LANES, LANES), BF16),
             pltpu.VMEM((3, 2, 8, CAP), F32),
@@ -462,11 +588,11 @@
             pltpu.VMEM((3, 2, COLUMNS, CAP), BF16),
             pltpu.VMEM((3, 2, 8, CAP), F32),
             pltpu.VMEM((3, 2, 8, CAP), F32),
-            pltpu.SemaphoreType.DMA((18,)),
-            pltpu.SemaphoreType.DMA((18,)),
+            pltpu.SemaphoreType.DMA((2 * len(OFFSETS) + 6,)),
+            pltpu.SemaphoreType.DMA((2 * len(OFFSETS) + 6,)),
         ],
         compiler_params=pltpu.CompilerParams(
-            collective_id=0, has_side_effects=True, vmem_limit_bytes=40 * 1024 * 1024
+            collective_id=0, has_side_effects=True, vmem_limit_bytes=64 * 1024 * 1024
         ),
         cost_estimate=pl.CostEstimate(flops=10**9, bytes_accessed=10**6, transcendentals=0),
         name="collisions",

time: 73.9 us -> 56.7 us (0.77)
  the two profiles are of different devices: /device:TPU:2 before, /device:TPU:1 now
where the time goes in v2:
time: 56.7 us; the launch traced here: 56.5 us
  Pallas kernels  52.9 us (93%)
  local copies, waits for them, and re-layouts  2.95 us (5%)
  between operations  0.65 us (1%)
    pallas_call x1, Pallas kernels, per_device(): pl.pallas_call(kernel, out_shape=(jax.ShapeDtypeStruct((3, solvent), F32)...  52.9 us
    unnamed x7, local copies, waits for them, and re-layouts  2.95 us

profile of v2, /device:TPU:1, one launch (start us, length us, event | category | flops | bytes accessed | tf_op | source)
XLA Modules:
  0.0 56.5 jit_solution(13035015521210140941)
XLA Ops:
  0.6 52.9 %collisions.1 = (f32[3,10240]{1,0:T(4,128)}, f32[3,1024]{1,0:T(4,128)}, f32[3,3,2,256]{3,2,1,0:T(2,128)}) custom-call(s32[2,3]{1,0:T(2,128)} %shift_hbm.1, s32[2,3]{1,0:T(2,128)} %bitcast.13, f32[3,10240]{1,0:T(4,128)} %velocity_hbm.1, s32[3,2,10240]{2,1,0:T(2,128)} %bitcast.9, f32[3,1024]{1,0:T(4,128)} %bead_velocity_hbm.1, f32[1,1024]{1,0:T(1,128)} %bitcast.12, ...), custom_call_target="tpu_custom_call" | custom-call | flops 1000000000 | bytes 1000000 | tf_op jit(solution)/shard_map/collisions/pallas_call | solution.py:548
  53.5 0.0 copy-start.1
  53.5 1.6 %copy.16 = f32[3,10240]{1,0:T(4,128)} copy(f32[3,10240]{1,0:T(4,128)} %get-tuple-element.12) | data formatting | bytes 245760
  55.1 0.0 copy-done.1
  55.1 0.0 copy-start
  55.1 0.6 %copy.17 = f32[3,1024]{1,0:T(4,128)} copy(f32[3,1024]{1,0:T(4,128)S(1)} %copy-done.1) | data formatting | bytes 24576
  55.7 0.1 copy-done
  55.9 0.6 %copy.18 = f32[3,2,3,256]{3,1,2,0:T(2,128)} copy(f32[3,2,3,256]{3,1,2,0:T(2,128)S(1)} %bitcast.8) | data formatting | bytes 36864
Async XLA Ops:
  53.5 1.6 %copy-start.1 = (f32[3,1024]{1,0:T(4,128)S(1)}, f32[3,1024]{1,0:T(4,128)}, u32[]{:S(2)}) copy-start(f32[3,1024]{1,0:T(4,128)} %get-tuple-element.13) | copy-start | bytes 36868
  55.1 0.7 %copy-start = (f32[3,3,2,256]{3,2,1,0:T(2,128)S(1)}, f32[3,3,2,256]{3,2,1,0:T(2,128)}, u32[]{:S(2)}) copy-start(f32[3,3,2,256]{3,2,1,0:T(2,128)} %get-tuple-element.8) | copy-start | bytes 55300

commit v3 on v2

--- a/solution.py
+++ b/solution.py
@@ -218,7 +218,7 @@
             onehots[step, :, here] = one_hot(column)
             return carry
 
-        lax.fori_loop(first, first + number, body, 0)
+        lax.fori_loop(first, first + number, body, 0, unroll=number)
 
     def place_beads(step):
         here = pl.ds(solvent, beads)
@@ -441,7 +441,7 @@
         deposit(0, here, moving[:, here])
         return carry
 
-    lax.fori_loop(0, chunks, first_deposit, 0)
+    lax.fori_loop(0, chunks, first_deposit, 0, unroll=chunks)
 
     def between_first():
         place(1, 0, solvent_chunks)
@@ -458,7 +458,7 @@
         deposit(1, here, moved)
         return carry
 
-    lax.fori_loop(0, chunks, turn, 0)
+    lax.fori_loop(0, chunks, turn, 0, unroll=chunks)
 
     tiles = solvent // LANES
 
@@ -479,7 +479,7 @@
             ).astype(BF16)
             return carry
 
-        lax.fori_loop(0, tiles // 2, fill, 0)
+        lax.fori_loop(0, tiles // 2, fill, 0, unroll=8)
 
         def pick(d, carry):
             for side in range(2):
@@ -500,13 +500,13 @@
                 leave_onehot[d, side] = one_hot(chosen[3:4].astype(I32))
             return carry
 
-        lax.fori_loop(0, 3, pick, 0)
+        lax.fori_loop(0, 3, pick, 0, unroll=3)
 
     exchange(1, between_second)
 
     slot = lanes_of((8, CAP))
     travels = []
-    for d in range(3):
+    for d in (2, 0, 1):
         for side in range(2):
             gathered = jnp.dot(
                 results[...], leave_onehot[d, side], preferred_element_type=F32
@@ -528,7 +528,7 @@
         velocity_out[:, here] = gather_collide(1, here)[0:3]
         return carry
 
-    lax.fori_loop(0, solvent_chunks, finish, 0)
+    lax.fori_loop(0, solvent_chunks, finish, 0, unroll=solvent_chunks)
     bead_out[...] = gather_collide(1, pl.ds(solvent, beads))[0:3]
 
     for travel in travels:
@@ -536,6 +536,18 @@
     for d in range(3):
         for side in range(2):
             arrivals_out[d, :, side, :] = leave_recv[d, side, 0:3, :]
+
+
+def write(*refs):
+    sems = refs[-1]
+    count = len(refs) // 2
+    copies = [
+        pltpu.make_async_copy(refs[i], refs[count + i], sems.at[i]) for i in range(count)
+    ]
+    for copy in copies:
+        copy.start()
+    for copy in copies:
+        copy.wait()
 
 
 def per_device(
@@ -548,9 +560,9 @@
     velocity_out, bead_out, arrivals = pl.pallas_call(
         kernel,
         out_shape=(
-            jax.ShapeDtypeStruct((3, solvent), F32),
-            jax.ShapeDtypeStruct((3, beads), F32),
-            jax.ShapeDtypeStruct((3, 3, 2, CAP), F32),
+            pltpu.VMEM((3, solvent), F32),
+            pltpu.VMEM((3, beads), F32),
+            pltpu.VMEM((3, 3, 2, CAP), F32),
         ),
         in_specs=[pl.BlockSpec(memory_space=pltpu.HBM)] * 10,
         out_specs=(vmem, vmem, vmem),
@@ -592,7 +604,7 @@
             pltpu.SemaphoreType.DMA((2 * len(OFFSETS) + 6,)),
         ],
         compiler_params=pltpu.CompilerParams(
-            collective_id=0, has_side_effects=True, vmem_limit_bytes=64 * 1024 * 1024
+            collective_id=0, has_side_effects=True, vmem_limit_bytes=62 * 1024 * 1024
         ),
         cost_estimate=pl.CostEstimate(flops=10**9, bytes_accessed=10**6, transcendentals=0),
         name="collisions",
@@ -608,6 +620,16 @@
         leave_index,
         jnp.asarray(rotation_table()),
     )
+    made = (velocity_out, bead_out, arrivals)
+    velocity_out, bead_out, arrivals = pl.pallas_call(
+        write,
+        out_shape=tuple(jax.ShapeDtypeStruct(x.shape, x.dtype) for x in made),
+        in_specs=[vmem] * 3,
+        out_specs=(pl.BlockSpec(memory_space=pltpu.HBM),) * 3,
+        scratch_shapes=[pltpu.SemaphoreType.DMA((3,))],
+        compiler_params=pltpu.CompilerParams(vmem_limit_bytes=4 * 1024 * 1024),
+        name="write_results",
+    )(*made)
     return velocity_out, bead_out, jnp.transpose(arrivals, (0, 2, 1, 3))
 
 

time: 56.7 us -> 49.1 us (0.87)
  Pallas kernels: 52.9 us -> 48.3 us
  local copies, waits for them, and re-layouts: 2.95 us -> 0 us
    pallas_call x1 -> x2, Pallas kernels: 52.9 us -> 48.3 us  [the longest x1 47.6 us: per_device(): pl.pallas_call(kernel, out_shape=(pltpu.VMEM((3, solvent), F32), pltpu.VM...]
    unnamed x7 -> x0, local copies, waits for them, and re-layouts: 2.95 us -> none
where the time goes in v3:
time: 49.1 us; the launch traced here: 48.9 us
  Pallas kernels  48.3 us (98%)
  between operations  0.64 us (1%)
    pallas_call x1, Pallas kernels, per_device(): pl.pallas_call(kernel, out_shape=(pltpu.VMEM((3, solvent), F32), pltpu.VM...  47.6 us

profile of v3, /device:TPU:1, one launch (start us, length us, event | category | flops | bytes accessed | tf_op | source)
XLA Modules:
  0.0 48.9 jit_solution(18053628397197376903)
XLA Ops:
  0.6 47.6 %collisions.1 = (f32[3,10240]{1,0:T(4,128)S(1)}, f32[3,1024]{1,0:T(4,128)S(1)}, f32[3,3,2,256]{3,2,1,0:T(2,128)S(1)}) custom-call(s32[2,3]{1,0:T(2,128)} %shift_hbm.1, s32[2,3]{1,0:T(2,128)} %bitcast.13, f32[3,10240]{1,0:T(4,128)} %velocity_hbm.1, s32[3,2,10240]{2,1,0:T(2,128)} %bitcast.8, f32[3,1024]{1,0:T(4,128)} %bead_velocity_hbm.1, f32[1,1024]{1,0:T(1,128)} %bitcast.12, ...), custom_call_target="tpu_custom_call" | custom-call | flops 1000000000 | bytes 1000000 | tf_op jit(solution)/shard_map/collisions/pallas_call | solution.py:560
  48.2 0.7 %write_results.1 = (f32[3,10240]{1,0:T(4,128)}, f32[3,1024]{1,0:T(4,128)}, f32[3,3,2,256]{3,2,1,0:T(2,128)}) custom-call(f32[3,10240]{1,0:T(4,128)S(1)} %get-tuple-element.9.refs_0_, f32[3,1024]{1,0:T(4,128)S(1)} %get-tuple-element.10.refs_1_, f32[3,3,2,256]{3,2,1,0:T(2,128)S(1)} %get-tuple-element.11.refs_2_), custom_call_target="tpu_custom_call" | custom-call | tf_op jit(solution)/shard_map/write_results/pallas_call | solution.py:624

commit v4 on v3

--- a/solution.py
+++ b/solution.py
@@ -41,12 +41,9 @@
     return table
 
 
-OFFSETS = [
-    (dx, dy, dz)
-    for dx in (-1, 0, 1)
-    for dy in (-1, 0, 1)
-    for dz in (-1, 0, 1)
-    if (dx, dy, dz) != (0, 0, 0)
+PLANE = [(dx, dy) for dx in (-1, 0, 1) for dy in (-1, 0, 1)]
+OFFSETS = [(dx, dy, dz) for dz in (-1, 1) for dx, dy in PLANE] + [
+    (dx, dy, 0) for dx, dy in PLANE if (dx, dy) != (0, 0)
 ]
 EDGES = [(dx, dy) for dx in (-1, 0, 1) for dy in (-1, 1)]
 
@@ -114,10 +111,14 @@
 
 
 def collide(moving, layer, gathered, tables):
-    n = moving.shape[1]
     chosen = gathered[0:8]
     for z in range(1, 17):
         chosen = jnp.where(layer == z, gathered[8 * z : 8 * z + 8], chosen)
+    return rotate(moving, chosen, tables)
+
+
+def rotate(moving, chosen, tables):
+    n = moving.shape[1]
     mean = chosen + pltpu.roll(chosen, 4, 0)
     axis = jnp.broadcast_to(mean[3:4], (8, n)).astype(I32)
     relative = moving - mean
@@ -143,7 +144,7 @@
     bead_position_ref, rot_ref, leave_ref, table_ref, load_sem,
     moving, weight, cols, lays, onehots, totals, cells, results,
     send_z, send_y, send_x, recv_edge, recv_line, recv_z, recv_y, recv_x,
-    leave_table, leave_moving, leave_layer, leave_onehot, leave_send, leave_recv,
+    leave_table, leave_moving, leave_layer, leave_column, leave_onehot, leave_send, leave_recv,
     send_sem, recv_sem,
 ):
     solvent = velocity_ref.shape[1]
@@ -156,7 +157,7 @@
     def device_at(offset):
         where = {}
         for name, step_by in zip(names, offset):
-            if step_by:
+            if step_by is not None and not (isinstance(step_by, int) and step_by == 0):
                 size, me = lax.axis_size(name), lax.axis_index(name)
                 where[name] = lax.rem(me + size + step_by, size)
         return where
@@ -251,11 +252,15 @@
         below = jnp.concatenate([by_layer, jnp.zeros((1, WIDE), F32)], axis=0)
         return jnp.where(offset[2] > 0, above, below)
 
-    def exchange(step, between):
+    last = lax.axis_index("gz") & 1
+    first = 1 - last
+
+    def exchange(step, between, early=None):
         axes = own_axes(step)
         row8w = rows_of((8, WIDE))
         row8 = rows_of((8, LANES))
         cells[:, :, COLUMNS:WIDE] = jnp.zeros((LAYERS, 8, WIDE - COLUMNS), F32)
+        cells[17] = jnp.zeros((8, WIDE), F32)
 
         def settle(z):
             part = totals[8 * z : 8 * z + 8, :]
@@ -382,8 +387,6 @@
                     )
 
         def entry_of(z):
-            if z == 17:
-                return jnp.zeros((8, WIDE), F32)
             full = cells[z]
             full = jnp.where((row8w >= 4) & (row8w < 7), pltpu.roll(full, 4, 0), full)
             mean = full / jnp.maximum(full[3:4], 1.0)
@@ -393,15 +396,22 @@
 
         def finish_pair(z):
             pair = jnp.concatenate([entry_of(z), entry_of(z + 1)], axis=0).astype(BF16)
-            results[8 * z : 8 * z + 16, :] = pair[:, 0:COLUMNS]
+            where = 8 * z if isinstance(z, int) else pl.multiple_of(8 * z, 16)
+            results[pl.ds(where, 16), :] = pair[:, 0:COLUMNS]
 
         for z in range(2, 16, 2):
             finish_pair(z)
 
-        for offset, travel in travels.items():
-            if offset[2] != 0:
-                travel.wait()
-        for side in range(2):
+        def collect(side):
+            for dx, dy in PLANE:
+                if dy:
+                    landed = recv_edge.at[step, side, EDGES.index((dx, dy))]
+                elif dx:
+                    landed = recv_line.at[step, side, (1 + dx) // 2]
+                else:
+                    landed = recv_z.at[step, side]
+                number = len(OFFSETS) * step + 9 * (1 - side) + PLANE.index((-dx, -dy))
+                remote(landed, landed, number, (0, 0, 1)).wait_recv()
             face = recv_z[step, side]
             lane1 = lanes_of((1, LANES))
             place10 = lax.rem(lane1, 10)
@@ -425,6 +435,15 @@
             cells[16 * side, :, LANES:WIDE] += far
             finish_pair(16 * side)
 
+        collect(first)
+        if early is not None:
+            finish_pair(16 * last)
+            early()
+        collect(last)
+        for offset, travel in travels.items():
+            if offset[2] != 0:
+                travel.wait_send()
+
     tables = [table_ref[c] for c in range(3)]
 
     def gather_collide(step, here):
@@ -497,31 +516,41 @@
                     chosen = jnp.where(tile == i, found[8 * i : 8 * i + 8], chosen)
                 leave_moving[d, side] = chosen + pltpu.roll(chosen, 4, 0)
                 leave_layer[d, side] = chosen[7:8].astype(I32)
+                leave_column[d, side] = chosen[3:4]
                 leave_onehot[d, side] = one_hot(chosen[3:4].astype(I32))
             return carry
 
         lax.fori_loop(0, 3, pick, 0, unroll=3)
 
-    exchange(1, between_second)
-
+    row8 = rows_of((8, CAP))
     slot = lanes_of((8, CAP))
+
+    def leave(d, side, shared=None):
+        gathered = jnp.dot(results[...], leave_onehot[d, side], preferred_element_type=F32)
+        before, layer = leave_moving[d, side], leave_layer[d, side]
+        moved = collide(before, layer, gathered, tables)
+        unused = 0.0
+        if shared is not None:
+            open_ = jnp.broadcast_to(layer, (8, CAP)) == shared
+            mark = jnp.where(open_, leave_column[d, side], -1.0)
+            moved = jnp.where(row8 == 3, mark, jnp.where(open_, before, moved))
+            unused = jnp.where(row8 == 3, -1.0, 0.0)
+        leave_send[d, side] = jnp.where(slot < count_ref[side, d], moved, unused)
+        step_by = 2 * side - 1
+        offset = tuple(step_by if axis == d else None for axis in range(3))
+        travel = remote(
+            leave_send.at[d, side], leave_recv.at[d, 1 - side], leave_number(d, side), offset
+        )
+        travel.start()
+        return travel
+
+    def leave_number(d, side):
+        return 2 * len(OFFSETS) + 2 * d + side
+
     travels = []
-    for d in (2, 0, 1):
-        for side in range(2):
-            gathered = jnp.dot(
-                results[...], leave_onehot[d, side], preferred_element_type=F32
-            )
-            moved = collide(leave_moving[d, side], leave_layer[d, side], gathered, tables)
-            leave_send[d, side] = jnp.where(slot < count_ref[side, d], moved, 0.0)
-            offset = tuple(2 * side - 1 if axis == d else 0 for axis in range(3))
-            travel = remote(
-                leave_send.at[d, side],
-                leave_recv.at[d, 1 - side],
-                2 * len(OFFSETS) + 2 * d + side,
-                offset,
-            )
-            travel.start()
-            travels.append(travel)
+    exchange(1, between_second, lambda: travels.append(leave(2, last, 16 * last)))
+    for d, side in ((0, 0), (0, 1), (2, first), (1, 0), (1, 1)):
+        travels.append(leave(d, side))
 
     def finish(i, carry):
         here = pl.ds(pl.multiple_of(i * CHUNK, CHUNK), CHUNK)
@@ -531,11 +560,27 @@
     lax.fori_loop(0, solvent_chunks, finish, 0, unroll=solvent_chunks)
     bead_out[...] = gather_collide(1, pl.ds(solvent, beads))[0:3]
 
+    arrived = leave_recv.at[2, last]
+    remote(arrived, arrived, leave_number(2, first), (0, 0, 1)).wait_recv()
+    got = leave_recv[2, last]
+    mark = got[3:4]
+    shared = jnp.dot(
+        results[pl.ds(pl.multiple_of(128 * last, 16), 16), :],
+        one_hot(mark.astype(I32)),
+        preferred_element_type=F32,
+    )
+    got = jnp.where(mark >= 0.0, rotate(got, shared[0:8], tables), got)
+    arrived = leave_recv.at[2, first]
+    remote(arrived, arrived, leave_number(2, last), (0, 0, 1)).wait_recv()
+    for side in range(2):
+        arrivals_out[2, :, side, :] = jnp.where(last == side, got, leave_recv[2, side])[0:3]
+    for d in range(2):
+        for side in range(2):
+            arrived = leave_recv.at[d, side]
+            remote(arrived, arrived, leave_number(d, 1 - side), (0, 0, 1)).wait_recv()
+            arrivals_out[d, :, side, :] = leave_recv[d, side, 0:3, :]
     for travel in travels:
-        travel.wait()
-    for d in range(3):
-        for side in range(2):
-            arrivals_out[d, :, side, :] = leave_recv[d, side, 0:3, :]
+        travel.wait_send()
 
 
 def write(*refs):
@@ -597,6 +642,7 @@
             pltpu.VMEM((8 * solvent // LANES, LANES), BF16),
             pltpu.VMEM((3, 2, 8, CAP), F32),
             pltpu.VMEM((3, 2, 1, CAP), I32),
+            pltpu.VMEM((3, 2, 1, CAP), F32),
             pltpu.VMEM((3, 2, COLUMNS, CAP), BF16),
             pltpu.VMEM((3, 2, 8, CAP), F32),
             pltpu.VMEM((3, 2, 8, CAP), F32),

time: 49.1 us -> 47.3 us (0.963)
  Pallas kernels: 48.3 us -> 46.6 us
    pallas_call x1, Pallas kernels: 47.6 us -> 45.9 us  [per_device(): pl.pallas_call(kernel, out_shape=(pltpu.VMEM((3, solvent), F32), pltpu.VM...]
where the time goes in v4:
time: 47.3 us; the launch traced here: 47.2 us
  Pallas kernels  46.6 us (99%)
  between operations  0.64 us (1%)
    pallas_call x1, Pallas kernels, per_device(): pl.pallas_call(kernel, out_shape=(pltpu.VMEM((3, solvent), F32), pltpu.VM...  45.9 us

profile of v4, /device:TPU:1, one launch (start us, length us, event | category | flops | bytes accessed | tf_op | source)
XLA Modules:
  0.0 47.2 jit_solution(14396132019355418428)
XLA Ops:
  0.6 45.9 %collisions.1 = (f32[3,10240]{1,0:T(4,128)S(1)}, f32[3,1024]{1,0:T(4,128)S(1)}, f32[3,3,2,256]{3,2,1,0:T(2,128)S(1)}) custom-call(s32[2,3]{1,0:T(2,128)} %shift_hbm.1, s32[2,3]{1,0:T(2,128)} %bitcast.13, f32[3,10240]{1,0:T(4,128)} %velocity_hbm.1, s32[3,2,10240]{2,1,0:T(2,128)} %bitcast.8, f32[3,1024]{1,0:T(4,128)} %bead_velocity_hbm.1, f32[1,1024]{1,0:T(1,128)} %bitcast.12, ...), custom_call_target="tpu_custom_call" | custom-call | flops 1000000000 | bytes 1000000 | tf_op jit(solution)/shard_map/collisions/pallas_call | solution.py:605
  46.5 0.7 %write_results.1 = (f32[3,10240]{1,0:T(4,128)}, f32[3,1024]{1,0:T(4,128)}, f32[3,3,2,256]{3,2,1,0:T(2,128)}) custom-call(f32[3,10240]{1,0:T(4,128)S(1)} %get-tuple-element.9.refs_0_, f32[3,1024]{1,0:T(4,128)S(1)} %get-tuple-element.10.refs_1_, f32[3,3,2,256]{3,2,1,0:T(2,128)S(1)} %get-tuple-element.11.refs_2_), custom_call_target="tpu_custom_call" | custom-call | tf_op jit(solution)/shard_map/write_results/pallas_call | solution.py:670

commit v5 on v4

--- a/solution.py
+++ b/solution.py
@@ -142,9 +142,10 @@
     velocity_out, bead_out, arrivals_out,
     shift_ref, count_ref, velocity_ref, position_ref, bead_velocity_ref, bead_mass_ref,
     bead_position_ref, rot_ref, leave_ref, table_ref, load_sem,
-    moving, weight, cols, lays, onehots, totals, cells, results,
+    moving, weight, cols, lays, onehots, turned_onehots, totals, cells, results,
     send_z, send_y, send_x, recv_edge, recv_line, recv_z, recv_y, recv_x,
     leave_table, leave_moving, leave_layer, leave_column, leave_onehot, leave_send, leave_recv,
+    ahead_send, ahead_recv,
     send_sem, recv_sem,
 ):
     solvent = velocity_ref.shape[1]
@@ -162,9 +163,16 @@
                 where[name] = lax.rem(me + size + step_by, size)
         return where
 
+    last = lax.axis_index("gz") & 1
+    first = 1 - last
+
     barrier = pltpu.get_barrier_semaphore()
-    for offset in OFFSETS:
-        pl.semaphore_signal(barrier, inc=1, device_id=device_at(offset), device_id_type=MESH)
+    for dz in (2 * last - 1, 0, 2 * first - 1):
+        for dx, dy in PLANE:
+            if dx or dy or not isinstance(dz, int):
+                pl.semaphore_signal(
+                    barrier, inc=1, device_id=device_at((dx, dy, dz)), device_id_type=MESH
+                )
 
     loads = [
         pltpu.make_async_copy(src, dst, load_sem.at[i])
@@ -231,9 +239,12 @@
 
     def deposit(step, here, moved):
         rows = deposit_rows(moved, weight[:, here], lays[step, :, here])
-        totals[...] += lax.dot_general(
-            rows, onehots[step, :, here], (((1,), (1,)), ((), ())), preferred_element_type=F32
-        )
+        if step == 0:
+            totals[...] += lax.dot_general(
+                rows, onehots[0, :, here], (((1,), (1,)), ((), ())), preferred_element_type=F32
+            )
+        else:
+            totals[...] += jnp.dot(rows, turned_onehots[here, :], preferred_element_type=F32)
 
     lane = lanes_of((8, LANES))
 
@@ -252,9 +263,6 @@
         below = jnp.concatenate([by_layer, jnp.zeros((1, WIDE), F32)], axis=0)
         return jnp.where(offset[2] > 0, above, below)
 
-    last = lax.axis_index("gz") & 1
-    first = 1 - last
-
     def exchange(step, between, early=None):
         axes = own_axes(step)
         row8w = rows_of((8, WIDE))
@@ -269,7 +277,8 @@
 
         settle(0)
         settle(16)
-        for side in range(2):
+
+        def pack_end(side):
             near, far = cells[16 * side, :, 0:LANES], cells[16 * side, :, LANES:WIDE]
             edge = lanes_from(far, lane + 32 - 10 * row8)
             edge = jnp.where((lane >= 10 * row8) & (lane < 10 * row8 + 10), edge, 0.0)
@@ -284,33 +293,33 @@
             send_z[step, side, 5:9] = near[0:4]
             send_z[step, side, 9:10] = near[7:8]
 
+        plane_travels, end_travels = [], []
+
+        def send(src, dst, number, offset):
+            travel = remote(src, dst, len(OFFSETS) * step + number, offset)
+            travel.start()
+            return travel
+
+        def send_end(side):
+            for dx, dy in sorted(PLANE, key=lambda place: -abs(place[1])):
+                if dy:
+                    src = send_z.at[step, side, pl.ds(2, 1)]
+                    dst = recv_edge.at[step, 1 - side, EDGES.index((-dx, -dy))]
+                elif dx:
+                    src = send_z.at[step, side, pl.ds(1 + dx, 3)]
+                    dst = recv_line.at[step, 1 - side, (1 - dx) // 2]
+                else:
+                    src = send_z.at[step, side, pl.ds(2, 8)]
+                    dst = recv_z.at[step, 1 - side]
+                number = 9 * side + PLANE.index((dx, dy))
+                end_travels.append(send(src, dst, number, (dx, dy, 2 * side - 1)))
+
+        pack_end(last)
         if step == 0:
             pl.semaphore_wait(barrier, len(OFFSETS))
-
-        travels = {}
-
-        def send(src, dst, offset):
-            travel = remote(src, dst, len(OFFSETS) * step + OFFSETS.index(offset), offset)
-            travel.start()
-            travels[offset] = travel
-
-        for side in range(2):
-            dz = 2 * side - 1
-            for dx in (-1, 0, 1):
-                for dy in (-1, 1):
-                    back = EDGES.index((-dx, -dy))
-                    send(
-                        send_z.at[step, side, pl.ds(2, 1)],
-                        recv_edge.at[step, 1 - side, back],
-                        (dx, dy, dz),
-                    )
-            for dx in (-1, 1):
-                send(
-                    send_z.at[step, side, pl.ds(1 + dx, 3)],
-                    recv_line.at[step, 1 - side, (1 - dx) // 2],
-                    (dx, 0, dz),
-                )
-            send(send_z.at[step, side, pl.ds(2, 8)], recv_z.at[step, 1 - side], (0, 0, dz))
+        send_end(last)
+        pack_end(first)
+        send_end(first)
 
         for z in range(1, 16):
             settle(z)
@@ -325,7 +334,14 @@
         for dx in (-1, 0, 1):
             for dy in (-1, 1):
                 back = EDGES.index((-dx, -dy))
-                send(send_y.at[step], recv_y.at[step, back], (dx, dy, 0))
+                plane_travels.append(
+                    send(
+                        send_y.at[step],
+                        recv_y.at[step, back],
+                        OFFSETS.index((dx, dy, 0)),
+                        (dx, dy, 0),
+                    )
+                )
 
         for group in range(6):
             packed_low = jnp.zeros((8, LANES), F32)
@@ -344,14 +360,21 @@
                     packed_high = jnp.where(inside, face_high, packed_high)
             send_x[step, 0, group] = packed_low
             send_x[step, 1, group] = packed_high
-        send(send_x.at[step, 0], recv_x.at[step, 1], (-1, 0, 0))
-        send(send_x.at[step, 1], recv_x.at[step, 0], (1, 0, 0))
+        for side in range(2):
+            offset = (2 * side - 1, 0, 0)
+            plane_travels.append(
+                send(
+                    send_x.at[step, side],
+                    recv_x.at[step, 1 - side],
+                    OFFSETS.index(offset),
+                    offset,
+                )
+            )
 
         between()
 
-        for offset, travel in travels.items():
-            if offset[2] == 0:
-                travel.wait()
+        for travel in plane_travels:
+            travel.wait()
         place12 = lax.rem(lane, 12)
         both_groups = []
         for group in range(2):
@@ -440,9 +463,8 @@
             finish_pair(16 * last)
             early()
         collect(last)
-        for offset, travel in travels.items():
-            if offset[2] != 0:
-                travel.wait_send()
+        for travel in end_travels:
+            travel.wait_send()
 
     tables = [table_ref[c] for c in range(3)]
 
@@ -465,6 +487,13 @@
     def between_first():
         place(1, 0, solvent_chunks)
         place_beads(1)
+
+        def transpose(i, carry):
+            here = pl.ds(pl.multiple_of(i * CHUNK, CHUNK), CHUNK)
+            turned_onehots[here, :] = onehots[1, :, here].T
+            return carry
+
+        lax.fori_loop(0, chunks, transpose, 0, unroll=chunks)
 
     exchange(0, between_first)
 
@@ -525,30 +554,37 @@
     row8 = rows_of((8, CAP))
     slot = lanes_of((8, CAP))
 
-    def leave(d, side, shared=None):
-        gathered = jnp.dot(results[...], leave_onehot[d, side], preferred_element_type=F32)
-        before, layer = leave_moving[d, side], leave_layer[d, side]
-        moved = collide(before, layer, gathered, tables)
-        unused = 0.0
-        if shared is not None:
-            open_ = jnp.broadcast_to(layer, (8, CAP)) == shared
-            mark = jnp.where(open_, leave_column[d, side], -1.0)
-            moved = jnp.where(row8 == 3, mark, jnp.where(open_, before, moved))
-            unused = jnp.where(row8 == 3, -1.0, 0.0)
-        leave_send[d, side] = jnp.where(slot < count_ref[side, d], moved, unused)
-        step_by = 2 * side - 1
-        offset = tuple(step_by if axis == d else None for axis in range(3))
-        travel = remote(
-            leave_send.at[d, side], leave_recv.at[d, 1 - side], leave_number(d, side), offset
-        )
+    def leave_number(d, side):
+        return 2 * len(OFFSETS) + 2 * d + side
+
+    def send_leaving(src, dst, number, d, side):
+        offset = tuple(2 * side - 1 if axis == d else None for axis in range(3))
+        travel = remote(src, dst, number, offset)
         travel.start()
         return travel
 
-    def leave_number(d, side):
-        return 2 * len(OFFSETS) + 2 * d + side
+    def leave(d, side):
+        gathered = jnp.dot(results[...], leave_onehot[d, side], preferred_element_type=F32)
+        moved = collide(leave_moving[d, side], leave_layer[d, side], gathered, tables)
+        leave_send[d, side] = jnp.where(slot < count_ref[side, d], moved, 0.0)
+        return send_leaving(
+            leave_send.at[d, side], leave_recv.at[d, 1 - side], leave_number(d, side), d, side
+        )
 
     travels = []
-    exchange(1, between_second, lambda: travels.append(leave(2, last, 16 * last)))
+
+    def ahead():
+        shared = jnp.broadcast_to(leave_layer[2, last], (8, CAP)) == 16 * last
+        shared &= slot < count_ref[last, 2]
+        mark = jnp.where(shared, leave_column[2, last], -1.0)
+        ahead_send[...] = jnp.where(row8 == 3, mark, leave_moving[2, last])
+        travels.append(send_leaving(ahead_send, ahead_recv, 2 * len(OFFSETS) + 6, 2, last))
+
+    def between_all():
+        between_second()
+        ahead()
+
+    exchange(1, between_all, lambda: travels.append(leave(2, last)))
     for d, side in ((0, 0), (0, 1), (2, first), (1, 0), (1, 1)):
         travels.append(leave(d, side))
 
@@ -560,16 +596,18 @@
     lax.fori_loop(0, solvent_chunks, finish, 0, unroll=solvent_chunks)
     bead_out[...] = gather_collide(1, pl.ds(solvent, beads))[0:3]
 
-    arrived = leave_recv.at[2, last]
-    remote(arrived, arrived, leave_number(2, first), (0, 0, 1)).wait_recv()
-    got = leave_recv[2, last]
+    remote(ahead_recv, ahead_recv, 2 * len(OFFSETS) + 6, (0, 0, 1)).wait_recv()
+    got = ahead_recv[...]
     mark = got[3:4]
     shared = jnp.dot(
         results[pl.ds(pl.multiple_of(128 * last, 16), 16), :],
         one_hot(mark.astype(I32)),
         preferred_element_type=F32,
     )
-    got = jnp.where(mark >= 0.0, rotate(got, shared[0:8], tables), got)
+    got = rotate(got, shared[0:8], tables)
+    arrived = leave_recv.at[2, last]
+    remote(arrived, arrived, leave_number(2, first), (0, 0, 1)).wait_recv()
+    got = jnp.where(mark >= 0.0, got, leave_recv[2, last])
     arrived = leave_recv.at[2, first]
     remote(arrived, arrived, leave_number(2, last), (0, 0, 1)).wait_recv()
     for side in range(2):
@@ -628,6 +666,7 @@
             pltpu.VMEM((2, 1, count), I32),
             pltpu.VMEM((2, 1, count), I32),
             pltpu.VMEM((2, COLUMNS, count), BF16),
+            pltpu.VMEM((count, COLUMNS), BF16),
             pltpu.VMEM((8 * LAYERS, COLUMNS), F32),
             pltpu.VMEM((LAYERS, 8, WIDE), F32),
             pltpu.VMEM((8 * LAYERS, COLUMNS), BF16),
@@ -646,8 +685,10 @@
             pltpu.VMEM((3, 2, COLUMNS, CAP), BF16),
             pltpu.VMEM((3, 2, 8, CAP), F32),
             pltpu.VMEM((3, 2, 8, CAP), F32),
-            pltpu.SemaphoreType.DMA((2 * len(OFFSETS) + 6,)),
-            pltpu.SemaphoreType.DMA((2 * len(OFFSETS) + 6,)),
+            pltpu.VMEM((8, CAP), F32),
+            pltpu.VMEM((8, CAP), F32),
+            pltpu.SemaphoreType.DMA((2 * len(OFFSETS) + 7,)),
+            pltpu.SemaphoreType.DMA((2 * len(OFFSETS) + 7,)),
         ],
         compiler_params=pltpu.CompilerParams(
             collective_id=0, has_side_effects=True, vmem_limit_bytes=62 * 1024 * 1024

time: 47.3 us -> 46.7 us (0.987)
  Pallas kernels: 46.6 us -> 45.9 us
    pallas_call x1, Pallas kernels: 45.9 us -> 45.2 us  [per_device(): pl.pallas_call(kernel, out_shape=(pltpu.VMEM((3, solvent), F32), pltpu.VM...]
where the time goes in v5:
time: 46.7 us; the launch traced here: 46.5 us
  Pallas kernels  45.9 us (98%)
  between operations  0.64 us (1%)
    pallas_call x1, Pallas kernels, per_device(): pl.pallas_call(kernel, out_shape=(pltpu.VMEM((3, solvent), F32), pltpu.VM...  45.2 us

profile of v5, /device:TPU:1, one launch (start us, length us, event | category | flops | bytes accessed | tf_op | source)
XLA Modules:
  0.0 46.5 jit_solution(389419951989970583)
XLA Ops:
  0.6 45.2 %collisions.1 = (f32[3,10240]{1,0:T(4,128)S(1)}, f32[3,1024]{1,0:T(4,128)S(1)}, f32[3,3,2,256]{3,2,1,0:T(2,128)S(1)}) custom-call(s32[2,3]{1,0:T(2,128)} %shift_hbm.1, s32[2,3]{1,0:T(2,128)} %bitcast.13, f32[3,10240]{1,0:T(4,128)} %velocity_hbm.1, s32[3,2,10240]{2,1,0:T(2,128)} %bitcast.8, f32[3,1024]{1,0:T(4,128)} %bead_velocity_hbm.1, f32[1,1024]{1,0:T(1,128)} %bitcast.12, ...), custom_call_target="tpu_custom_call" | custom-call | flops 1000000000 | bytes 1000000 | tf_op jit(solution)/shard_map/collisions/pallas_call | solution.py:643
  45.8 0.7 %write_results.1 = (f32[3,10240]{1,0:T(4,128)}, f32[3,1024]{1,0:T(4,128)}, f32[3,3,2,256]{3,2,1,0:T(2,128)}) custom-call(f32[3,10240]{1,0:T(4,128)S(1)} %get-tuple-element.9.refs_0_, f32[3,1024]{1,0:T(4,128)S(1)} %get-tuple-element.10.refs_1_, f32[3,3,2,256]{3,2,1,0:T(2,128)S(1)} %get-tuple-element.11.refs_2_), custom_call_target="tpu_custom_call" | custom-call | tf_op jit(solution)/shard_map/write_results/pallas_call | solution.py:711

commit v6 on v5

--- a/solution.py
+++ b/solution.py
@@ -111,9 +111,13 @@
 
 
 def collide(moving, layer, gathered, tables):
-    chosen = gathered[0:8]
-    for z in range(1, 17):
-        chosen = jnp.where(layer == z, gathered[8 * z : 8 * z + 8], chosen)
+    found = [gathered[8 * z : 8 * z + 8] for z in range(17)]
+    top = found.pop()
+    wide = jnp.broadcast_to(layer, (8, layer.shape[1]))
+    for bit in range(4):
+        odd = (wide & (1 << bit)) != 0
+        found = [jnp.where(odd, found[z + 1], found[z]) for z in range(0, len(found), 2)]
+    chosen = jnp.where(wide == 16, top, found[0])
     return rotate(moving, chosen, tables)
 
 
@@ -563,15 +567,26 @@
         travel.start()
         return travel
 
-    def leave(d, side):
-        gathered = jnp.dot(results[...], leave_onehot[d, side], preferred_element_type=F32)
-        moved = collide(leave_moving[d, side], leave_layer[d, side], gathered, tables)
-        leave_send[d, side] = jnp.where(slot < count_ref[side, d], moved, 0.0)
-        return send_leaving(
-            leave_send.at[d, side], leave_recv.at[d, 1 - side], leave_number(d, side), d, side
-        )
-
     travels = []
+
+    def leave(*faces):
+        found = [
+            jnp.dot(results[...], leave_onehot[face], preferred_element_type=F32)
+            for face in faces
+        ]
+        for (d, side), gathered in zip(faces, found):
+            moved = collide(leave_moving[d, side], leave_layer[d, side], gathered, tables)
+            leave_send[d, side] = jnp.where(slot < count_ref[side, d], moved, 0.0)
+        for d, side in faces:
+            travels.append(
+                send_leaving(
+                    leave_send.at[d, side],
+                    leave_recv.at[d, 1 - side],
+                    leave_number(d, side),
+                    d,
+                    side,
+                )
+            )
 
     def ahead():
         shared = jnp.broadcast_to(leave_layer[2, last], (8, CAP)) == 16 * last
@@ -584,9 +599,9 @@
         between_second()
         ahead()
 
-    exchange(1, between_all, lambda: travels.append(leave(2, last)))
-    for d, side in ((0, 0), (0, 1), (2, first), (1, 0), (1, 1)):
-        travels.append(leave(d, side))
+    exchange(1, between_all, lambda: leave((2, last)))
+    leave((0, 0), (0, 1))
+    leave((2, first), (1, 0), (1, 1))
 
     def finish(i, carry):
         here = pl.ds(pl.multiple_of(i * CHUNK, CHUNK), CHUNK)

time: 46.7 us -> 46.5 us (level)
  no operation moved by 1% of the time
where the time goes in v6:
time: 46.5 us; the launch traced here: 46.4 us
  Pallas kernels  45.8 us (98%)
  between operations  0.64 us (1%)
    pallas_call x1, Pallas kernels, per_device(): pl.pallas_call(kernel, out_shape=(pltpu.VMEM((3, solvent), F32), pltpu.VM...  45.1 us

profile of v6, /device:TPU:1, one launch (start us, length us, event | category | flops | bytes accessed | tf_op | source)
XLA Modules:
  0.0 46.4 jit_solution(10463864919307670752)
XLA Ops:
  0.6 45.1 %collisions.1 = (f32[3,10240]{1,0:T(4,128)S(1)}, f32[3,1024]{1,0:T(4,128)S(1)}, f32[3,3,2,256]{3,2,1,0:T(2,128)S(1)}) custom-call(s32[2,3]{1,0:T(2,128)} %shift_hbm.1, s32[2,3]{1,0:T(2,128)} %bitcast.13, f32[3,10240]{1,0:T(4,128)} %velocity_hbm.1, s32[3,2,10240]{2,1,0:T(2,128)} %bitcast.8, f32[3,1024]{1,0:T(4,128)} %bead_velocity_hbm.1, f32[1,1024]{1,0:T(1,128)} %bitcast.12, ...), custom_call_target="tpu_custom_call" | custom-call | flops 1000000000 | bytes 1000000 | tf_op jit(solution)/shard_map/collisions/pallas_call | solution.py:658
  45.7 0.7 %write_results.1 = (f32[3,10240]{1,0:T(4,128)}, f32[3,1024]{1,0:T(4,128)}, f32[3,3,2,256]{3,2,1,0:T(2,128)}) custom-call(f32[3,10240]{1,0:T(4,128)S(1)} %get-tuple-element.9.refs_0_, f32[3,1024]{1,0:T(4,128)S(1)} %get-tuple-element.10.refs_1_, f32[3,3,2,256]{3,2,1,0:T(2,128)S(1)} %get-tuple-element.11.refs_2_), custom_call_target="tpu_custom_call" | custom-call | tf_op jit(solution)/shard_map/write_results/pallas_call | solution.py:726

commit v7 on v6

--- a/solution.py
+++ b/solution.py
@@ -319,11 +319,11 @@
                 end_travels.append(send(src, dst, number, (dx, dy, 2 * side - 1)))
 
         pack_end(last)
-        if step == 0:
-            pl.semaphore_wait(barrier, len(OFFSETS))
-        send_end(last)
+        if step > 0:
+            send_end(last)
         pack_end(first)
-        send_end(first)
+        if step > 0:
+            send_end(first)
 
         for z in range(1, 16):
             settle(z)
@@ -335,17 +335,21 @@
                     turned = pltpu.roll(cells[z, :, LANES:WIDE], (12 * j - 32) % LANES, 1)
                     packed = jnp.where((lane >= 12 * j) & (lane < 12 * j + 10), turned, packed)
             send_y[step, group] = packed
-        for dx in (-1, 0, 1):
-            for dy in (-1, 1):
-                back = EDGES.index((-dx, -dy))
-                plane_travels.append(
-                    send(
-                        send_y.at[step],
-                        recv_y.at[step, back],
-                        OFFSETS.index((dx, dy, 0)),
-                        (dx, dy, 0),
+        def send_second():
+            for dx in (-1, 0, 1):
+                for dy in (-1, 1):
+                    back = EDGES.index((-dx, -dy))
+                    plane_travels.append(
+                        send(
+                            send_y.at[step],
+                            recv_y.at[step, back],
+                            OFFSETS.index((dx, dy, 0)),
+                            (dx, dy, 0),
+                        )
                     )
-                )
+
+        if step > 0:
+            send_second()
 
         for group in range(6):
             packed_low = jnp.zeros((8, LANES), F32)
@@ -364,6 +368,11 @@
                     packed_high = jnp.where(inside, face_high, packed_high)
             send_x[step, 0, group] = packed_low
             send_x[step, 1, group] = packed_high
+        if step == 0:
+            pl.semaphore_wait(barrier, len(OFFSETS))
+            send_end(last)
+            send_end(first)
+            send_second()
         for side in range(2):
             offset = (2 * side - 1, 0, 0)
             plane_travels.append(

time: 46.5 us -> 46.5 us (level)
  no operation moved by 1% of the time
where the time goes in v7:
time: 46.5 us; the launch traced here: 46.4 us
  Pallas kernels  45.8 us (98%)
  between operations  0.64 us (1%)
    pallas_call x1, Pallas kernels, per_device(): pl.pallas_call(kernel, out_shape=(pltpu.VMEM((3, solvent), F32), pltpu.VM...  45.1 us

profile of v7, /device:TPU:1, one launch (start us, length us, event | category | flops | bytes accessed | tf_op | source)
XLA Modules:
  0.0 46.4 jit_solution(8885610706436804081)
XLA Ops:
  0.6 45.1 %collisions.1 = (f32[3,10240]{1,0:T(4,128)S(1)}, f32[3,1024]{1,0:T(4,128)S(1)}, f32[3,3,2,256]{3,2,1,0:T(2,128)S(1)}) custom-call(s32[2,3]{1,0:T(2,128)} %shift_hbm.1, s32[2,3]{1,0:T(2,128)} %bitcast.13, f32[3,10240]{1,0:T(4,128)} %velocity_hbm.1, s32[3,2,10240]{2,1,0:T(2,128)} %bitcast.8, f32[3,1024]{1,0:T(4,128)} %bead_velocity_hbm.1, f32[1,1024]{1,0:T(1,128)} %bitcast.12, ...), custom_call_target="tpu_custom_call" | custom-call | flops 1000000000 | bytes 1000000 | tf_op jit(solution)/shard_map/collisions/pallas_call | solution.py:667
  45.7 0.7 %write_results.1 = (f32[3,10240]{1,0:T(4,128)}, f32[3,1024]{1,0:T(4,128)}, f32[3,3,2,256]{3,2,1,0:T(2,128)}) custom-call(f32[3,10240]{1,0:T(4,128)S(1)} %get-tuple-element.9.refs_0_, f32[3,1024]{1,0:T(4,128)S(1)} %get-tuple-element.10.refs_1_, f32[3,3,2,256]{3,2,1,0:T(2,128)S(1)} %get-tuple-element.11.refs_2_), custom_call_target="tpu_custom_call" | custom-call | tf_op jit(solution)/shard_map/write_results/pallas_call | solution.py:735
